TPU v7x, 256 devices: a whole 4x4x8 slice. The times are simulated.
256 devices in a mesh: gx: 16 (over x, y), gy: 16 (over z, core).
Axes of the slice: x: 4, y: 4, z: 8, core: 2. Of those that a mesh axis runs over, the one named last changes fastest.
Arguments:
- conserved_states: float32 [5, 256, 512, 128], P(None, 'gx', 'gy'), may hold values from -400 to 400
- thermal_level: float32 [256, 512, 128], P('gx', 'gy'), may hold values from 0.8 to 2.5
- spread_factors: float32 [5], replicated, may hold values from 0.5 to 2
Outputs:
- new_fields: float32 [5, 256, 512, 128], P(None, 'gx', 'gy')
All inputs are finite; a program needn't handle non-finite values.
Results may differ from a plain program's by a relative error of at most 0.0003.
Values sent between devices are 32-bit elements; how exact they have to be, the bound alone decides.
A program may use at most 128 MiB of HBM per device.

v0:
```python
import jax
import jax.numpy as jnp
from jax import lax
from jax.sharding import PartitionSpec as P

step_ratio = 5000.0
power_rule_mu = 0.7


def extended(block, sides, width):
    for axis, dim in sides:
        count = lax.axis_size(axis)
        forward = [(i, i + 1) for i in range(count - 1)]
        backward = [(target, source) for source, target in forward]
        low = lax.ppermute(
            lax.slice_in_dim(block, block.shape[dim] - width, None, axis=dim), axis, forward
        )
        high = lax.ppermute(lax.slice_in_dim(block, 0, width, axis=dim), axis, backward)
        block = jnp.concatenate([low, block, high], axis=dim)
    return block


def entering(array, axis, combine, identity, reverse):
    length, place = (lax.axis_size(axis), lax.axis_index(axis))
    everything = jax.tree.map(lambda part: lax.all_gather(part, axis), array)
    start = jax.tree.map(
        lambda part, zero: jnp.broadcast_to(jnp.asarray(zero, part.dtype), part.shape),
        array,
        identity,
    )

    def hop(k, before):
        at = length - 1 - k if reverse else k
        reached = at > place if reverse else at < place
        new = combine(before, jax.tree.map(lambda part: part[at], everything))
        return jax.tree.map(lambda a, b: jnp.where(reached, a, b), new, before)

    return lax.fori_loop(0, length, hop, start)


def thomas(lower_diagonal, main_diag, super_diag, source):

    def forward(state_now, items):
        upper_prev, value_prev = state_now
        low_item, main_item, upper_item, source_item = items
        pivots = main_item - low_item * upper_prev
        upper_next = upper_item / pivots
        value_next = (source_item - low_item * value_prev) / pivots
        return ((upper_next, value_next), (upper_next, value_next))

    start_state = (jnp.zeros_like(lower_diagonal[0]), jnp.zeros_like(source[0]))
    unused, (uppers, values) = lax.scan(
        forward, start_state, (lower_diagonal, main_diag, super_diag, source)
    )

    def backward(later_value, items):
        upper_item, value_entry = items
        current = value_entry - upper_item * later_value
        return (current, current)

    unused_last, solved = lax.scan(
        backward, jnp.zeros_like(source[0]), (uppers, values), reverse=True
    )
    return solved


def coefficients(faces, spread_factors):
    weights = step_ratio * spread_factors[None, :, None, None] * faces[:, None]
    return (weights, -weights[:-1], 1.0 + weights[:-1] + weights[1:], -weights[1:])


def local_block(moved, faces, spread_factors):
    weights, lower_diagonal, main_diag, super_diag = coefficients(faces, spread_factors)
    zero_rows = jnp.zeros_like(moved[1:])
    from_left = jnp.concatenate([weights[:1], zero_rows], axis=0)
    from_right = jnp.concatenate([zero_rows, weights[-1:]], axis=0)
    source = jnp.stack([moved, from_left, from_right], axis=1)
    solved = thomas(lower_diagonal[:, None], main_diag[:, None], super_diag[:, None], source)
    base, left_part, right_part = (solved[:, 0], solved[:, 1], solved[:, 2])
    block = (base[0], left_part[0], right_part[0], base[-1], left_part[-1], right_part[-1])
    return (base, left_part, right_part, block)


def combine_blocks(left_block, right_block):
    pivots = 1.0 - left_block[5] * right_block[1]
    inner_const = (left_block[3] + left_block[5] * right_block[0]) / pivots
    inner_left = left_block[4] / pivots
    inner_right = left_block[5] * right_block[2] / pivots
    next_const = right_block[0] + right_block[1] * inner_const
    following_left = right_block[1] * inner_left
    next_right = right_block[1] * inner_right + right_block[2]
    return (
        left_block[0] + left_block[2] * next_const,
        left_block[1] + left_block[2] * following_left,
        left_block[2] * next_right,
        right_block[3] + right_block[4] * inner_const,
        right_block[4] * inner_left,
        right_block[4] * inner_right + right_block[5],
    )


def combine_reversed(earlier_block, later_block):
    return combine_blocks(later_block, earlier_block)


def identity_block(sample):
    zeros_like = jnp.zeros_like(sample)
    ones_like = jnp.ones_like(sample)
    return (zeros_like, zeros_like, ones_like, zeros_like, ones_like, zeros_like)


def choose_blocks(flag, taken_block, other_block):
    return tuple(
        (
            jnp.where(flag, taken_item, other_item)
            for taken_item, other_item in zip(taken_block, other_block)
        )
    )


def fold_gathered(gathered, position, count, sample):

    def pick(ordinal):
        return tuple(
            (lax.dynamic_index_in_dim(member, ordinal, 0, keepdims=False) for member in gathered)
        )

    def downward(ordinal, state_now):
        merged = combine_blocks(state_now, pick(ordinal))
        return choose_blocks(ordinal < position, merged, state_now)

    def upward(ordinal, state_now):
        source_index = count - 1 - ordinal
        merged = combine_blocks(pick(source_index), state_now)
        return choose_blocks(source_index > position, merged, state_now)

    before = lax.fori_loop(0, count, downward, identity_block(sample))
    after = lax.fori_loop(0, count, upward, identity_block(sample))
    return (before, after)


def interface(block, before, after):
    alpha_term, beta_term = (before[3], before[5])
    gamma_term, delta_term = (after[0], after[1])
    first_diag = 1.0 - block[1] * beta_term
    first_cross = -block[2] * delta_term
    last_cross = -block[4] * beta_term
    last_diag = 1.0 - block[5] * delta_term
    first_source = block[0] + block[1] * alpha_term + block[2] * gamma_term
    last_source = block[3] + block[4] * alpha_term + block[5] * gamma_term
    determinant = first_diag * last_diag - first_cross * last_cross
    first_value = (first_source * last_diag - first_cross * last_source) / determinant
    last_value = (first_diag * last_source - last_cross * first_source) / determinant
    left_value = alpha_term + beta_term * first_value
    right_value = gamma_term + delta_term * last_value
    return (left_value, right_value)


def apply_values(base, left_part, right_part, left_value, right_value):
    return base + left_part * left_value[None] + right_part * right_value[None]


def finish(base, left_part, right_part, block, before, after):
    left_value, right_value = interface(block, before, after)
    return apply_values(base, left_part, right_part, left_value, right_value)


def shards(conserved_states, thermal_level, spread_factors):
    implicit_friction_advance = thermal_level**power_rule_mu
    padded = extended(implicit_friction_advance, (("gx", 0), ("gy", 1)), 1)
    position_x = lax.axis_index("gx")
    count_x = lax.axis_size("gx")
    position_y = lax.axis_index("gy")
    count_y = lax.axis_size("gy")
    moved = jnp.moveaxis(conserved_states, 1, 0)
    west = jnp.where(position_x == 0, implicit_friction_advance[0], padded[0, 1:-1])
    east = jnp.where(position_x == count_x - 1, implicit_friction_advance[-1], padded[-1, 1:-1])
    line_x = jnp.concatenate([west[None], implicit_friction_advance, east[None]], axis=0)
    faces_x = 0.5 * (line_x[:-1] + line_x[1:])
    base, left_part, right_part, block = local_block(moved, faces_x, spread_factors)
    gathered = (
        lax.all_gather(block[0][None], "gx", axis=0, tiled=True),
        lax.all_gather(block[1][None], "gx", axis=0, tiled=True),
        lax.all_gather(block[2][None], "gx", axis=0, tiled=True),
        lax.all_gather(block[3][None], "gx", axis=0, tiled=True),
        lax.all_gather(block[4][None], "gx", axis=0, tiled=True),
        lax.all_gather(block[5][None], "gx", axis=0, tiled=True),
    )
    before, after = fold_gathered(gathered, position_x, count_x, block[0])
    half_step = finish(base, left_part, right_part, block, before, after)
    south = jnp.where(position_y == 0, implicit_friction_advance[:, 0], padded[1:-1, 0])
    north = jnp.where(position_y == count_y - 1, implicit_friction_advance[:, -1], padded[1:-1, -1])
    line_y = jnp.concatenate([south[:, None], implicit_friction_advance, north[:, None]], axis=1)
    faces_y = jnp.moveaxis(0.5 * (line_y[:, :-1] + line_y[:, 1:]), 1, 0)
    across = jnp.transpose(half_step, (2, 1, 0, 3))
    base_y, left_y, right_y, block_y = local_block(across, faces_y, spread_factors)
    start_y = identity_block(block_y[0])
    below = entering(
        (block_y[0], block_y[1], block_y[2], block_y[3], block_y[4], block_y[5]),
        "gy",
        combine_blocks,
        start_y,
        False,
    )
    above = entering(
        (block_y[0], block_y[1], block_y[2], block_y[3], block_y[4], block_y[5]),
        "gy",
        combine_reversed,
        start_y,
        True,
    )
    solved = finish(base_y, left_y, right_y, block_y, below, above)
    return jnp.transpose(solved, (1, 2, 0, 3))


def solution(mesh):
    return jax.shard_map(
        shards,
        mesh=mesh,
        in_specs=(P(None, "gx", "gy", None), P("gx", "gy", None), P()),
        out_specs=P(None, "gx", "gy", None),
        check_vma=False,
    )
```

profile of v0, /device:TPU:1, one launch (start us, length us, event | category | flops | bytes accessed | tf_op | source)
XLA Modules:
  0.0 802.0 jit_solution(16608974110635933306)
XLA Ops:
  7.6 4.0 collective-permute-start
  16.5 2.0 select_bitcast_fusion.1
  18.4 2.4 pad_maximum_fusion
  20.9 2.4 broadcast.90.clone
  23.2 53.1 %while.136 = (s32[]{:T(128)}, f32[1,5,32,128]{3,2,1,0:T(8,128)S(1)}, f32[3,5,32,128]{3,2,1,0:T(8,128)S(1)}, f32[16,1,5,32,128]{4,3,2,1,0:T(8,128)}, f32[16,3,5,3...) while((s32[]{:T(128)}, f32[1,5,32,128]{3,2,1,0:T(8,128)S(1)}, ...), condition=%wide.region_1.2_spmd.clone, body=%wide.region_0.1_spmd.clone.sunk | while | flops 327683 | bytes 1803384 | solution.py:52
  76.3 2.4 broadcast.90
  78.7 43.0 %while.137 = (s32[]{:T(128)}, f32[3,5,32,128]{3,2,1,0:T(8,128)S(1)}, f32[16,3,5,32,128]{4,3,2,1,0:T(8,128)}, f32[16,3,5,32,128]{4,3,2,1,0:T(8,128)}, f32[16,1,5,...) while((s32[]{:T(128)}, f32[3,5,32,128]{3,2,1,0:T(8,128)S(1)}, ...), condition=%wide.region_3.4_spmd.clone, body=%wide.region_2.3_spmd.clone.sunk | while | flops 184324 | bytes 1228915 | solution.py:61
  79.6 1.8 bitcast_dynamic-update-slice_fusion.14
  82.3 1.8 bitcast_dynamic-update-slice_fusion.14
  85.0 1.8 bitcast_dynamic-update-slice_fusion.14
  93.1 1.8 bitcast_dynamic-update-slice_fusion.14
  98.4 1.8 bitcast_dynamic-update-slice_fusion.14
  101.1 1.8 bitcast_dynamic-update-slice_fusion.14
  106.5 1.8 bitcast_dynamic-update-slice_fusion.14
  109.2 1.8 bitcast_dynamic-update-slice_fusion.14
  111.9 1.8 bitcast_dynamic-update-slice_fusion.14
  114.6 1.8 bitcast_dynamic-update-slice_fusion.14
  117.3 1.8 bitcast_dynamic-update-slice_fusion.14
  119.9 1.8 bitcast_dynamic-update-slice_fusion.14
  121.7 1.9 fusion.80
  126.9 5.5 collective-permute-start.2
  132.4 1.9 collective-permute-start.3
  134.5 6.3 copy.19
  141.4 2.3 select_bitcast_fusion
  143.7 33.2 %all-gather.19.cloned.1.call-done = f32[16,1,5,32,128]{4,3,2,1,0:T(8,128)} async-done(((f32[1,1,5,32,128]{4,3,2,1,0:T(8,128)}), f32[16,1,5,32,128]{4,3,2,1,0:T(8,128)}) %all-gather.19.cloned.1.call-update) | async-done | bytes 1310736 | tf_op jit(solution)/shard_map/all_gather | solution.py:185
  176.9 50.3 %all-gather.21.cloned.1.call-done = f32[16,1,5,32,128]{4,3,2,1,0:T(8,128)} async-done(((f32[1,1,5,32,128]{4,3,2,1,0:T(8,128)}), f32[16,1,5,32,128]{4,3,2,1,0:T(8,128)}) %all-gather.21.cloned.1.call-update) | async-done | bytes 1310736 | tf_op jit(solution)/shard_map/all_gather | solution.py:186
  227.2 50.3 %all-gather.23.cloned.1.call-done = f32[16,1,5,32,128]{4,3,2,1,0:T(8,128)} async-done(((f32[1,1,5,32,128]{4,3,2,1,0:T(8,128)}), f32[16,1,5,32,128]{4,3,2,1,0:T(8,128)}) %all-gather.23.cloned.1.call-update) | async-done | bytes 1310736 | tf_op jit(solution)/shard_map/all_gather | solution.py:182
  277.5 50.2 %all-gather.25.cloned.1.call-done = f32[16,1,5,32,128]{4,3,2,1,0:T(8,128)} async-done(((f32[1,1,5,32,128]{4,3,2,1,0:T(8,128)}), f32[16,1,5,32,128]{4,3,2,1,0:T(8,128)}) %all-gather.25.cloned.1.call-update) | async-done | bytes 1310736 | tf_op jit(solution)/shard_map/all_gather | solution.py:183
  327.7 50.2 %all-gather.27.cloned.1.call-done = f32[16,1,5,32,128]{4,3,2,1,0:T(8,128)} async-done(((f32[1,1,5,32,128]{4,3,2,1,0:T(8,128)}), f32[16,1,5,32,128]{4,3,2,1,0:T(8,128)}) %all-gather.27.cloned.1.call-update) | async-done | bytes 1310736 | tf_op jit(solution)/shard_map/all_gather | solution.py:184
  377.8 50.2 %all-gather.29.cloned.1.call-done = f32[16,1,5,32,128]{4,3,2,1,0:T(8,128)} async-done(((f32[1,1,5,32,128]{4,3,2,1,0:T(8,128)}), f32[16,1,5,32,128]{4,3,2,1,0:T(8,128)}) %all-gather.29.cloned.1.call-update) | async-done | bytes 1310736 | tf_op jit(solution)/shard_map/all_gather | solution.py:187
  428.0 19.2 %while.139 = (s32[]{:T(128)}, f32[5,32,128]{2,1,0:T(8,128)S(1)}, f32[5,32,128]{2,1,0:T(8,128)S(1)}, s32[]{:T(128)}, f32[16,5,32,128]{3,2,1,0:T(8,128)}, /*index=...) while((s32[]{:T(128)}, f32[5,32,128]{2,1,0:T(8,128)S(1)}, ...), condition=%wide.region_7.8_spmd.clone, body=%wide.region_6.7_spmd.clone.sunk | while | flops 348168 | bytes 819403 | solution.py:138
  447.2 19.0 %while.138 = (s32[]{:T(128)}, f32[5,32,128]{2,1,0:T(8,128)S(1)}, f32[5,32,128]{2,1,0:T(8,128)S(1)}, s32[]{:T(128)}, f32[16,5,32,128]{3,2,1,0:T(8,128)}, /*index=...) while((s32[]{:T(128)}, f32[5,32,128]{2,1,0:T(8,128)S(1)}, ...), condition=%wide.region_5.6_spmd.clone, body=%wide.region_4.5_spmd.clone.sunk | while | flops 307204 | bytes 819341 | solution.py:137
  467.5 2.4 fusion.53
  470.0 2.2 pad_maximum_fusion.1
  472.1 2.2 broadcast.87.clone
  474.3 97.6 %while.140 = (s32[]{:T(128)}, f32[1,5,16,128]{3,2,1,0:T(8,128)S(1)}, f32[3,5,16,128]{3,2,1,0:T(8,128)S(1)}, f32[32,1,5,16,128]{4,3,2,1,0:T(8,128)}, f32[32,3,5,1...) while((s32[]{:T(128)}, f32[1,5,16,128]{3,2,1,0:T(8,128)S(1)}, ...), condition=%wide.region_9.10_spmd.clone, body=%wide.region_8.9_spmd.clone.sunk | while | flops 163843 | bytes 902264 | solution.py:52
  571.9 2.2 broadcast.87
  574.1 76.8 %while.141 = (s32[]{:T(128)}, f32[3,5,16,128]{3,2,1,0:T(8,128)S(1)}, f32[32,3,5,16,128]{4,3,2,1,0:T(8,128)}, f32[32,3,5,16,128]{4,3,2,1,0:T(8,128)}, f32[32,1,5,...) while((s32[]{:T(128)}, f32[3,5,16,128]{3,2,1,0:T(8,128)S(1)}, ...), condition=%wide.region_11.12_spmd.clone, body=%wide.region_10.11_spmd.clone.sunk | while | flops 92164 | bytes 614515 | solution.py:61
  651.8 5.2 copy.25
  656.9 20.6 %all-gather.6 = f32[16,1,5,16,128]{4,3,2,1,0:T(8,128)S(1)} all-gather(f32[1,1,5,16,128]{4,3,2,1,0:T(8,128)S(1)} %get-tuple-element.1541), channel_id=8, replica_groups=mesh['gx'=16,'gy'=16] {'gy'}, dimensions={0}, use_global_device_ids=true | all-gather | bytes 696320 | tf_op jit(solution)/shard_map/all_gather | solution.py:25
  677.5 16.8 %all-gather.7 = f32[16,1,5,16,128]{4,3,2,1,0:T(8,128)S(1)} all-gather(f32[1,1,5,16,128]{4,3,2,1,0:T(8,128)S(1)} %get-tuple-element.1539), channel_id=9, replica_groups=mesh['gx'=16,'gy'=16] {'gy'}, dimensions={0}, use_global_device_ids=true | all-gather | bytes 696320 | tf_op jit(solution)/shard_map/all_gather | solution.py:25
  694.3 17.0 %all-gather.8 = f32[16,1,5,16,128]{4,3,2,1,0:T(8,128)S(1)} all-gather(f32[1,1,5,16,128]{4,3,2,1,0:T(8,128)S(1)} %get-tuple-element.1540), channel_id=10, replica_groups=mesh['gx'=16,'gy'=16] {'gy'}, dimensions={0}, use_global_device_ids=true | all-gather | bytes 696320 | tf_op jit(solution)/shard_map/all_gather | solution.py:25
  711.3 16.8 %all-gather.9 = f32[16,1,5,16,128]{4,3,2,1,0:T(8,128)S(1)} all-gather(f32[1,1,5,16,128]{4,3,2,1,0:T(8,128)S(1)} %get-tuple-element.1543), channel_id=11, replica_groups=mesh['gx'=16,'gy'=16] {'gy'}, dimensions={0}, use_global_device_ids=true | all-gather | bytes 696320 | tf_op jit(solution)/shard_map/all_gather | solution.py:25
  728.1 17.0 %all-gather.10 = f32[16,1,5,16,128]{4,3,2,1,0:T(8,128)S(1)} all-gather(f32[1,1,5,16,128]{4,3,2,1,0:T(8,128)S(1)} %get-tuple-element.1542), channel_id=12, replica_groups=mesh['gx'=16,'gy'=16] {'gy'}, dimensions={0}, use_global_device_ids=true | all-gather | bytes 696320 | tf_op jit(solution)/shard_map/all_gather | solution.py:25
  745.1 18.2 %all-gather.11 = f32[16,1,5,16,128]{4,3,2,1,0:T(8,128)} all-gather(f32[1,1,5,16,128]{4,3,2,1,0:T(8,128)S(1)} %get-tuple-element.1544), channel_id=13, replica_groups=mesh['gx'=16,'gy'=16] {'gy'}, dimensions={0}, use_global_device_ids=true | all-gather | bytes 696320 | tf_op jit(solution)/shard_map/all_gather | solution.py:25
  763.3 13.6 %while.143 = (s32[]{:T(128)}, f32[5,16,128]{2,1,0:T(8,128)S(1)}, f32[5,16,128]{2,1,0:T(8,128)S(1)}, s32[]{:T(128)}, f32[16,5,16,128]{3,2,1,0:T(8,128)S(1)}, /*in...) while((s32[]{:T(128)}, f32[5,16,128]{2,1,0:T(8,128)S(1)}, ...), condition=%wide.region_15.16_spmd.clone, body=%wide.region_14.15_spmd.clone.sunk | while | flops 174088 | bytes 409803 | solution.py:38
  777.0 13.5 %while.142 = (s32[]{:T(128)}, f32[5,16,128]{2,1,0:T(8,128)S(1)}, f32[5,16,128]{2,1,0:T(8,128)S(1)}, s32[]{:T(128)}, f32[16,5,16,128]{3,2,1,0:T(8,128)S(1)}, /*in...) while((s32[]{:T(128)}, f32[5,16,128]{2,1,0:T(8,128)S(1)}, ...), condition=%wide.region_13.14_spmd.clone, body=%wide.region_12.13_spmd.clone.sunk | while | flops 153604 | bytes 409741 | solution.py:38
  791.4 3.7 fusion.48
  (300 shorter events, 325.3 us)
Async XLA Ops:
  6.5 170.4 %all-gather.19.cloned.1.call-start = ((), (), s32[]{:S(2)}) async-start(), calls=%async_computation | async-start | bytes 1392640 | tf_op jit(solution)/shard_map/all_gather | solution.py:185
  7.6 7.4 collective-permute-start
  11.7 4.5 collective-permute-start.1
  15.0 1.4 copy-start.1
  123.6 103.6 %all-gather.21.cloned.1.call-start = ((), (), s32[]{:S(2)}) async-start(), calls=%async_computation.1 | async-start | bytes 1392640 | tf_op jit(solution)/shard_map/all_gather | solution.py:186
  124.4 153.2 %all-gather.23.cloned.1.call-start = ((), (), s32[]{:S(2)}) async-start(), calls=%async_computation.2 | async-start | bytes 1392640 | tf_op jit(solution)/shard_map/all_gather | solution.py:182
  125.1 202.6 %all-gather.25.cloned.1.call-start = ((), (), s32[]{:S(2)}) async-start(), calls=%async_computation.3 | async-start | bytes 1392640 | tf_op jit(solution)/shard_map/all_gather | solution.py:183
  125.7 252.2 %all-gather.27.cloned.1.call-start = ((), (), s32[]{:S(2)}) async-start(), calls=%async_computation.4 | async-start | bytes 1392640 | tf_op jit(solution)/shard_map/all_gather | solution.py:184
  126.3 301.7 %all-gather.29.cloned.1.call-start = ((), (), s32[]{:S(2)}) async-start(), calls=%async_computation.5 | async-start | bytes 1392640 | tf_op jit(solution)/shard_map/all_gather | solution.py:187
  126.9 13.9 %collective-permute-start.2 = (f32[18,1,128]{2,1,0:T(1,128)S(1)}, f32[18,1,128]{2,1,0:T(1,128)S(1)}, u32[]{:S(2)}, u32[]{:S(2)}) collective-permute-start(f32[18,1,128]{2,1,0:T(1,128)S(1)} %get-tuple-element.1560), channel_id=1, source_target_pairs={{0,1},{1,2},{2,3},{3,4},{4,5},{5,6},{6,7},{7,8},{8,9},{9,10},{10,1... | collective-permute-start | bytes 27656 | tf_op jit(solution)/shard_map/ppermute | solution.py:15
  132.4 8.3 %collective-permute-start.3 = (f32[18,1,128]{2,1,0:T(1,128)S(1)}, f32[18,1,128]{2,1,0:T(1,128)S(1)}, u32[]{:S(2)}, u32[]{:S(2)}) collective-permute-start(f32[18,1,128]{2,1,0:T(1,128)S(1)} %get-tuple-element.1559), channel_id=1, source_target_pairs={{1,0},{2,1},{3,2},{4,3},{5,4},{6,5},{7,6},{8,7},{9,8},{10,9},{11,1... | collective-permute-start | bytes 27656 | tf_op jit(solution)/shard_map/ppermute | solution.py:18
  140.8 0.7 copy-start
Sparse Core Ops, SparseCore 0:
  123.7 53.1 all-gather.18
  179.4 47.7 all-gather.20
  229.7 47.7 all-gather.22
  279.9 47.7 all-gather.24
  330.0 47.7 all-gather.26
  380.2 47.7 all-gather.28
where the time goes:
time: 814 us; the launch traced here: 802 us
  other arithmetic  313 us (38%)
  waiting for transfers between devices  288 us (35%)
  blocking collectives  106 us (13%)
  local copies, waits for them, and re-layouts  65.6 us (8%)
  between operations  13.8 us (2%)
  starting transfers between devices  13 us (2%)
    dynamic_update_slice x144, other arithmetic, thomas(): lax.scan(forward, start_state, (lower_diagonal, main_diag, super_diag, so...  231 us
    all_gather x6, blocking collectives, entering(): everything = jax.tree.map(lambda part: lax.all_gather(part, axis), array)  106 us
    all_gather x1, waiting for transfers between devices, shards(): lax.all_gather(block[0][None], 'gx', axis=0, tiled=True)  50.3 us
    all_gather x1, waiting for transfers between devices, shards(): lax.all_gather(block[4][None], 'gx', axis=0, tiled=True)  50.3 us
    all_gather x1, waiting for transfers between devices, shards(): lax.all_gather(block[1][None], 'gx', axis=0, tiled=True)  50.2 us
    all_gather x1, waiting for transfers between devices, shards(): lax.all_gather(block[5][None], 'gx', axis=0, tiled=True)  50.2 us
    all_gather x1, waiting for transfers between devices, shards(): lax.all_gather(block[2][None], 'gx', axis=0, tiled=True)  50.2 us
    mul x48, local copies, waits for them, and re-layouts, backward(): current = value_entry - upper_item * later_value  39.3 us
  transfers between devices with their start and end apart: 10, of which 7 were waited for; matrix products, arithmetic and copies ran while one was open for 1% of the time, Pallas kernels for 0%

commit v1 on v0

v1 whole, which is shorter than its diff:
```python
import jax
import jax.numpy as jnp
from jax import lax
from jax.experimental import pallas as pl
from jax.experimental.pallas import tpu as pltpu
from jax.sharding import PartitionSpec as P

MESH = pl.DeviceIdType.MESH
FIELDS, NX, NY, LANES = 5, 16, 32, 128
PEERS = 16
ROWS = NX * NY
XM, XR, XV, YM, YR, YV = range(6)
SHARE = {XM: 40, XR: 24, XV: 24, YM: 24, YR: 16, YV: 16}


def ring(step, size):
    return min(step, size - step)


X_STEPS = sorted(
    [(a, b) for a in range(4) for b in range(4) if (a, b) != (0, 0)],
    key=lambda s: -(ring(s[0], 4) + ring(s[1], 4)),
)
Y_STEPS = sorted(
    [(a, b) for a in range(8) for b in range(2) if (a, b) != (0, 0)],
    key=lambda s: -ring(s[0], 8),
)


def partners(axis, gx, gy):
    if axis == "gx":
        a, b = gx // 4, gx % 4
        return [(((a + i) % 4) * 4 + (b + j) % 4, gy) for i, j in X_STEPS]
    a, b = gy // 2, gy % 2
    return [(gx, ((a + i) % 8) * 2 + (b + j) % 2) for i, j in Y_STEPS]


def rows(start, count):
    return pl.ds(start, count)


def chain_matrix(mass, link, wall_low, wall_high, half):
    sides = []
    last = 2 * half - 1
    for low in (True, False):
        at = (lambda j: j) if low else (lambda j: last - j)
        edge = (lambda j: link(j)) if low else (lambda j: link(last - j - 1))
        m = mass(at(0)) + (wall_low if low else wall_high)
        steps = []
        for j in range(half - 1):
            e = edge(j)
            p = 1.0 / (m + e)
            h = e * p
            steps.append((p, h))
            m = mass(at(j + 1)) + h * m
        sides.append((steps, m))
    w = link(half - 1)
    m_low, m_high = sides[0][1], sides[1][1]
    inverse = 1.0 / (m_low * m_high + w * (m_low + m_high))
    middle = ((m_high + w) * inverse, w * inverse, (m_low + w) * inverse)
    return sides[0][0], sides[1][0], middle


def chain_solve(parts, right, half):
    low, high, (a, b, c) = parts
    last = 2 * half - 1
    ends, kept = [], []
    for steps, at in ((low, lambda j: j), (high, lambda j: last - j)):
        r = right(at(0))
        q = []
        for j, (p, h) in enumerate(steps):
            q.append(p * r)
            r = right(at(j + 1)) + h * r
        ends.append(r)
        kept.append(q)
    values = [None] * (2 * half)
    values[half - 1] = a * ends[0] + b * ends[1]
    values[half] = b * ends[0] + c * ends[1]
    for j in range(half - 2, -1, -1):
        values[j] = kept[0][j] + low[j][1] * values[j + 1]
        values[last - j] = kept[1][j] + high[j][1] * values[last - j - 1]
    return values


def kernel(
    fields_hbm, level_hbm, spread, out,
    field, level, visc, xg, xh, xq, xa, xb, xp, half, yg, yh, yq, ya, yb, yp,
    s_xm, s_xr, s_xv, s_ym, s_yr, s_yv, r_xm, r_xr, r_xv, r_ym, r_yr, r_yv,
    chain_p, chain_h, send_sem, recv_sem, in_sem,
):
    gx, gy = lax.axis_index("gx"), lax.axis_index("gy")
    sends = (s_xm, s_xr, s_xv, s_ym, s_yr, s_yv)
    recvs = (r_xm, r_xr, r_xv, r_ym, r_yr, r_yv)
    everyone = partners("gx", gx, gy) + partners("gy", gx, gy)

    barrier = pltpu.get_barrier_semaphore()
    for device in everyone:
        pl.semaphore_signal(barrier, inc=1, device_id=device, device_id_type=MESH)
    level_in = pltpu.make_async_copy(level_hbm, level, in_sem.at[0])
    fields_in = pltpu.make_async_copy(fields_hbm, field, in_sem.at[1])
    level_in.start()
    fields_in.start()

    def axis_of(what):
        return "gx" if what in (XM, XR, XV) else "gy"

    def send(what):
        axis, size = axis_of(what), SHARE[what]
        me = gx if axis == "gx" else gy
        for device in partners(axis, gx, gy):
            peer = device[0] if axis == "gx" else device[1]
            pltpu.make_async_remote_copy(
                src_ref=sends[what].at[rows(pl.multiple_of(peer * size, 8), size)],
                dst_ref=recvs[what].at[rows(pl.multiple_of(me * size, 8), size)],
                send_sem=send_sem.at[what],
                recv_sem=recv_sem.at[what],
                device_id=device,
                device_id_type=MESH,
            ).start()
        mine = rows(pl.multiple_of(me * size, 8), size)
        recvs[what][mine] = sends[what][mine]

    def total(what):
        part = rows(0, (PEERS - 1) * SHARE[what])
        return pltpu.make_async_remote_copy(
            src_ref=sends[what].at[part],
            dst_ref=recvs[what].at[part],
            send_sem=send_sem.at[what],
            recv_sem=recv_sem.at[what],
            device_id=everyone[0],
            device_id_type=MESH,
        )

    rate = [2500.0 * spread[f] for f in range(FIELDS)]
    zero = jnp.zeros((16, LANES), jnp.float32)
    one = jnp.ones((16, LANES), jnp.float32)

    for ref, size, used in ((s_xm, 40, 34), (s_xr, 24, 20), (s_xv, 24, 20)):
        for row in range(used, size):
            ref[pl.ds(row, 16, stride=size)] = zero
    for ref, size, spare in ((s_ym, 24, (6, 7, 14, 15, 21, 22, 23)), (s_yr, 16, (5, 6, 7, 13, 14, 15))):
        for row in spare:
            ref[pl.ds(row, 16, stride=size)] = zero
    r_xr[rows(PEERS * SHARE[XR], 8)] = zero[:8]

    level_in.wait()

    def power(t, carry):
        at = rows(pl.multiple_of(t * 64, 64), 64)
        visc[at] = jnp.exp(0.7 * jnp.log(level[at]))
        return carry

    lax.fori_loop(0, ROWS // 64, power, 0)
    fields_in.wait()

    def x_row(f, i, s):
        return rows(pl.multiple_of(f * ROWS + i * NY + s * 16, 16), 16)

    def x_visc(i, s):
        return visc[rows(pl.multiple_of(i * NY + s * 16, 16), 16)]

    for s in range(2):
        nu0, nu1 = x_visc(0, s), x_visc(1, s)
        start = (
            nu1,
            tuple(rate[f] * (nu0 + nu1) for f in range(FIELDS)),
            (one,) * FIELDS,
            (one,) * FIELDS,
            tuple(field[x_row(f, 1, s)] for f in range(FIELDS)),
            tuple(field[x_row(f, 0, s)] for f in range(FIELDS)),
        )

        def forward(i, state, s=s):
            nu, edge, mass, first, right, first_right = state
            nu_next = x_visc(i + 1, s)
            face = nu + nu_next
            out_state = ([], [], [], [], [])
            for f in range(FIELDS):
                e, m, r = edge[f], mass[f], right[f]
                w = rate[f] * face
                p = 1.0 / (e + w + m)
                g, h = e * p, w * p
                at = x_row(f, i, s)
                xg[at] = g
                xh[at] = h
                xq[at] = p * r
                for box, item in zip(
                    out_state,
                    (g * w, 1.0 + h * m, first[f] + g * m, field[x_row(f, i + 1, s)] + h * r, first_right[f] + g * r),
                ):
                    box.append(item)
            return (nu_next,) + tuple(tuple(box) for box in out_state)

        nu, edge, mass, first, right, first_right = lax.fori_loop(1, NX - 1, forward, start)
        for f in range(FIELDS):
            for v, value in enumerate((first[f], mass[f], edge[f])):
                base = v * 8 + 2 * f + s if f < 4 else 24 + 2 * v + s
                s_xm[pl.ds(base, 16, stride=40)] = value
            for v, value in enumerate((first_right[f], right[f])):
                base = v * 8 + 2 * f + s if f < 4 else 16 + 2 * v + s
                s_xr[pl.ds(base, 16, stride=24)] = value
        s_xm[pl.ds(30 + s, 16, stride=40)] = nu0
        s_xm[pl.ds(32 + s, 16, stride=40)] = nu

    pl.semaphore_wait(barrier, len(everyone))
    send(XM)
    send(XR)

    def y_visc(j):
        return visc[pl.ds(j, 16, stride=NY)]

    def y_row(f, j):
        return rows(pl.multiple_of((f * NY + j) * 16, 16), 16)

    nu0, nu1 = y_visc(0), y_visc(1)
    start = (nu1, tuple(rate[f] * (nu0 + nu1) for f in range(FIELDS)), (one,) * FIELDS, (one,) * FIELDS)

    def forward(j, state):
        nu, edge, mass, first = state
        nu_next = y_visc(j + 1)
        face = nu + nu_next
        out_state = ([], [], [])
        for f in range(FIELDS):
            e, m = edge[f], mass[f]
            w = rate[f] * face
            p = 1.0 / (e + w + m)
            g, h = e * p, w * p
            at = y_row(f, j)
            yg[at] = g
            yh[at] = h
            yq[at] = p
            for box, item in zip(out_state, (g * w, 1.0 + h * m, first[f] + g * m)):
                box.append(item)
        return (nu_next,) + tuple(tuple(box) for box in out_state)

    nu, edge, mass, first = lax.fori_loop(1, NY - 1, forward, start)
    for f in range(FIELDS):
        for v, value in enumerate((first[f], mass[f], edge[f])):
            s_ym[pl.ds(v * 8 + f, 16, stride=24)] = value
    s_ym[pl.ds(5, 16, stride=24)] = nu0
    s_ym[pl.ds(13, 16, stride=24)] = nu
    send(YM)

    for s in range(2):
        for f in range(FIELDS):
            for i, ends in ((0, (one, zero)), (NX - 1, (zero, one))):
                at = x_row(f, i, s)
                xa[at], xb[at], xp[at] = ends[0], ends[1], zero

        def backward(k, state, s=s):
            i = NX - 2 - k
            new = []
            for f in range(FIELDS):
                a, b, p = state[f]
                at = x_row(f, i, s)
                h = xh[at]
                a, b, p = xg[at] + h * a, h * b, xq[at] + h * p
                xa[at], xb[at], xp[at] = a, b, p
                new.append((a, b, p))
            return tuple(new)

        lax.fori_loop(0, NX - 2, backward, ((zero, one, zero),) * FIELDS)

    line = lax.broadcasted_iota(jnp.int32, (16, LANES), 0)
    odd = line % 2 == 1
    rate_x = jnp.full((16, LANES), rate[FIELDS - 1], jnp.float32)
    for f in range(4):
        rate_x = jnp.where(line // 2 == f, rate[f], rate_x)

    def pack(ref, k, size, low, high):
        return jnp.concatenate([ref[rows(k * size + low, 8)], ref[rows(k * size + high, 8)]], axis=0)

    def x_mass(j):
        v = j % 2
        return pack(r_xm, j // 2, 40, 8 * v, 24 + 2 * v)

    def x_end_visc(k, v):
        base = k * 40 + 30 + 2 * v
        return jnp.where(odd, r_xm[rows(base + 1, 1)], r_xm[rows(base, 1)])

    def x_link(j):
        k = j // 2
        if j % 2 == 0:
            return pack(r_xm, k, 40, 16, 28)
        return rate_x * (x_end_visc(k, 1) + x_end_visc(k + 1, 0))

    total(XM).wait_recv()
    parts = chain_matrix(
        x_mass, x_link, 2.0 * rate_x * x_end_visc(0, 0), 2.0 * rate_x * x_end_visc(PEERS - 1, 1), PEERS
    )
    total(XR).wait_recv()
    solved = chain_solve(parts, lambda j: pack(r_xr, j // 2, 24, 8 * (j % 2), 16 + 2 * (j % 2)), PEERS)
    for k in range(PEERS):
        for v in range(2):
            s_xv[rows(k * 24 + 8 * v, 8)] = solved[2 * k + v][:8]
            s_xv[rows(k * 24 + 16 + 2 * v, 2)] = solved[2 * k + v][8:10]
    send(XV)

    def natural(f, j):
        return pl.ds(f * ROWS + j, 16, stride=NY)

    for f in range(FIELDS):
        for j, ends in ((0, (one, zero)), (NY - 1, (zero, one))):
            at = natural(f, j)
            ya[at], yb[at], yp[at] = ends[0], ends[1], zero

    def backward(k, state):
        j = NY - 2 - k
        new = []
        for f in range(FIELDS):
            a, b = state[f]
            at = y_row(f, j)
            h = yh[at]
            a, b = yg[at] + h * a, h * b
            ya[natural(f, j)], yb[natural(f, j)] = a, b
            new.append((a, b))
        return tuple(new)

    lax.fori_loop(0, NY - 2, backward, ((zero, one),) * FIELDS)

    rate_y = jnp.full((8, LANES), rate[FIELDS - 1], jnp.float32)
    line = lax.broadcasted_iota(jnp.int32, (8, LANES), 0)
    for f in range(4):
        rate_y = jnp.where(line == f, rate[f], rate_y)

    def y_end_visc(k, v):
        return r_ym[rows(k * 24 + 5 + 8 * v, 1)]

    def y_link(j):
        k = j // 2
        if j % 2 == 0:
            return r_ym[rows(k * 24 + 16, 8)]
        return rate_y * (y_end_visc(k, 1) + y_end_visc(k + 1, 0))

    total(YM).wait_recv()
    low, high, middle = chain_matrix(
        lambda j: r_ym[rows((j // 2) * 24 + 8 * (j % 2), 8)],
        y_link,
        2.0 * rate_y * y_end_visc(0, 0),
        2.0 * rate_y * y_end_visc(PEERS - 1, 1),
        PEERS,
    )
    for side, steps in enumerate((low, high)):
        for j, (p, h) in enumerate(steps):
            chain_p[rows((side * PEERS + j) * 8, 8)] = p
            chain_h[rows((side * PEERS + j) * 8, 8)] = h

    total(XV).wait_recv()
    for f in range(FIELDS):
        low_end, high_end = [], []
        for s in range(2):
            base = (2 * f + s, 8 + 2 * f + s) if f < 4 else (16 + s, 18 + s)
            low_end.append(r_xv[pl.ds(base[0], 16, stride=24)])
            high_end.append(r_xv[pl.ds(base[1], 16, stride=24)])
        low_end = jnp.concatenate(low_end, axis=0)
        high_end = jnp.concatenate(high_end, axis=0)

        def finish_x(i, carry, f=f, low_end=low_end, high_end=high_end):
            at = rows(pl.multiple_of(f * ROWS + i * NY, NY), NY)
            value = xp[at] + xa[at] * low_end + xb[at] * high_end
            half[at] = value
            s_yr[rows(i * 16 + f, 1)] = jnp.sum(ya[at] * value, axis=0, keepdims=True)
            s_yr[rows(i * 16 + 8 + f, 1)] = jnp.sum(yb[at] * value, axis=0, keepdims=True)
            return carry

        lax.fori_loop(0, NX, finish_x, 0)
    send(YR)

    def forward(j, right):
        new = []
        for f in range(FIELDS):
            at = y_row(f, j)
            yg[at] = yq[at] * right[f]
            new.append(half[natural(f, j + 1)] + yh[at] * right[f])
        return tuple(new)

    lax.fori_loop(1, NY - 1, forward, tuple(half[natural(f, 1)] for f in range(FIELDS)))

    def backward(k, state):
        j = NY - 2 - k
        new = []
        for f in range(FIELDS):
            at = y_row(f, j)
            p = yg[at] + yh[at] * state[f]
            yp[natural(f, j)] = p
            new.append(p)
        return tuple(new)

    lax.fori_loop(0, NY - 2, backward, (zero,) * FIELDS)

    total(YR).wait_recv()
    parts = tuple(
        [
            (chain_p[rows((side * PEERS + j) * 8, 8)], chain_h[rows((side * PEERS + j) * 8, 8)])
            for j in range(PEERS - 1)
        ]
        for side in range(2)
    ) + (middle,)
    solved = chain_solve(parts, lambda j: r_yr[rows((j // 2) * 16 + 8 * (j % 2), 8)], PEERS)
    for k in range(PEERS):
        for v in range(2):
            s_yv[rows(k * 16 + 8 * v, 8)] = solved[2 * k + v]
    send(YV)

    total(YV).wait_recv()

    def finish_y(i, carry):
        for f in range(FIELDS):
            at = rows(pl.multiple_of(f * ROWS + i * NY, NY), NY)
            low_end, high_end = r_yv[rows(i * 16 + f, 1)], r_yv[rows(i * 16 + 8 + f, 1)]
            out[at] = yp[at] + ya[at] * low_end + yb[at] * high_end
        return carry

    lax.fori_loop(0, NX, finish_y, 0)
    for what in range(6):
        total(what).wait_send()


def shards(conserved_states, thermal_level, spread_factors):
    def buffer(count):
        return pltpu.VMEM((count, LANES), jnp.float32)

    whole = buffer(FIELDS * ROWS)
    messages = [buffer(PEERS * SHARE[what]) for what in range(6)]
    arrivals = [buffer(PEERS * SHARE[what] + 8) for what in range(6)]
    solved = pl.pallas_call(
        kernel,
        out_shape=jax.ShapeDtypeStruct((FIELDS * ROWS, LANES), jnp.float32),
        in_specs=[
            pl.BlockSpec(memory_space=pl.ANY),
            pl.BlockSpec(memory_space=pl.ANY),
            pl.BlockSpec(memory_space=pltpu.SMEM),
        ],
        out_specs=pl.BlockSpec(memory_space=pltpu.VMEM),
        scratch_shapes=[whole, buffer(ROWS), buffer(ROWS)]
        + [whole] * 13
        + messages
        + arrivals
        + [
            buffer(2 * PEERS * 8),
            buffer(2 * PEERS * 8),
            pltpu.SemaphoreType.DMA((6,)),
            pltpu.SemaphoreType.DMA((6,)),
            pltpu.SemaphoreType.DMA((2,)),
        ],
        compiler_params=pltpu.CompilerParams(
            collective_id=0, has_side_effects=True, vmem_limit_bytes=48 * 1024 * 1024
        ),
    )(
        conserved_states.reshape(FIELDS * ROWS, LANES),
        thermal_level.reshape(ROWS, LANES),
        spread_factors,
    )
    return solved.reshape(conserved_states.shape)


def solution(mesh):
    return jax.shard_map(
        shards,
        mesh=mesh,
        in_specs=(P(None, "gx", "gy", None), P("gx", "gy", None), P()),
        out_specs=P(None, "gx", "gy", None),
        check_vma=False,
    )
```

time: 814 us -> 40.9 us (0.05); the launches traced: 802 us -> 40.8 us
  other arithmetic: 313 us -> 0 us
  waiting for transfers between devices: 288 us -> 0 us
  blocking collectives: 106 us -> 0 us
  local copies, waits for them, and re-layouts: 65.6 us -> 3.98 us
  Pallas kernels: 0 us -> 36.8 us
  between operations: 13.8 us -> 0.01 us
  starting transfers between devices: 13 us -> 0 us
    all_gather x6 -> x0, waiting for transfers between devices: 284 us -> none  [the longest x1 50.3 us: shards(): lax.all_gather(block[0][None], 'gx', axis=0, tiled=True)]
    dynamic_update_slice x144 -> x0, other arithmetic: 231 us -> none  [thomas(): lax.scan(forward, start_state, (lower_diagonal, main_diag, super_diag, so...]
    all_gather x6 -> x0, blocking collectives: 106 us -> none  [entering(): everything = jax.tree.map(lambda part: lax.all_gather(part, axis), array)]
    select_n x66 -> x0, other arithmetic: 63.7 us -> none  [the longest x32 37.4 us: choose_blocks(): jnp.where(flag, taken_item, other_item)]
    mul x48 -> x0, local copies, waits for them, and re-layouts: 39.3 us -> none  [backward(): current = value_entry - upper_item * later_value]
    pallas_call x0 -> x1, Pallas kernels: none -> 36.8 us  [shards(): pl.pallas_call(kernel, out_shape=jax.ShapeDtypeStruct((FIELDS * ROWS, LAN...]
    ppermute x4 -> x0, starting transfers between devices: 12.8 us -> none  [the longest x2 9.57 us: extended(): lax.ppermute(lax.slice_in_dim(block, block.shape[dim] - width, None, axis...]
    while x2 -> x0, local copies, waits for them, and re-layouts: 11.5 us -> none  [thomas(): lax.scan(backward, jnp.zeros_like(source[0]), (uppers, values), reverse=T...]
  transfers between devices with their start and end apart: 10 -> 0, of which waited for: 7 -> 0; matrix products, arithmetic and copies ran while one was open for 1% -> 0% of each run, Pallas kernels for 0% -> 0%
where the time goes in v1:
time: 40.9 us; the launch traced here: 40.8 us
  Pallas kernels  36.8 us (90%)
  local copies, waits for them, and re-layouts  3.98 us (10%)
    pallas_call x1, Pallas kernels, shards(): pl.pallas_call(kernel, out_shape=jax.ShapeDtypeStruct((FIELDS * ROWS, LAN...  36.8 us
    unnamed x7, local copies, waits for them, and re-layouts  3.98 us

profile of v1, /device:TPU:1, one launch (start us, length us, event | category | flops | bytes accessed | tf_op | source)
XLA Modules:
  0.0 40.8 jit_solution(2276300381651186749)
XLA Ops:
  0.0 0.0 copy-start
  0.0 1.3 %copy-done = f32[5,16,32,128]{3,2,1,0:T(8,128)S(1)} copy-done((f32[5,16,32,128]{3,2,1,0:T(8,128)S(1)}, f32[5,16,32,128]{3,2,1,0:T(8,128)}, u32[]{:S(2)}) %copy-start) | copy-done | bytes 1310744
  1.3 0.0 copy-start.1
  1.3 0.9 %copy-done.1 = f32[16,32,128]{2,1,0:T(8,128)S(1)} copy-done((f32[16,32,128]{2,1,0:T(8,128)S(1)}, f32[16,32,128]{2,1,0:T(8,128)}, u32[]{:S(2)}) %copy-start.1) | copy-done | bytes 262168
  2.3 0.0 copy-start.2
  2.3 0.7 %copy-done.2 = f32[5]{0:T(128)S(1)} copy-done((f32[5]{0:T(128)S(1)}, f32[5]{0:T(128)}, u32[]{:S(2)}) %copy-start.2) | copy-done | bytes 44
  2.9 36.8 %shard_map.37 = f32[2560,128]{1,0:T(8,128)S(1)} custom-call(f32[2560,128]{1,0:T(8,128)S(1)} %bitcast.4, f32[512,128]{1,0:T(8,128)S(1)} %bitcast.5, f32[5]{0:T(128)S(1)} %copy-done.2), custom_call_target="tpu_custom_call" | custom-call | tf_op jit(solution)/shard_map/pallas_call | solution.py:426
  39.7 1.1 %copy.5 = f32[5,16,32,128]{3,2,1,0:T(8,128)} copy(f32[5,16,32,128]{3,2,1,0:T(8,128)S(1)} %bitcast.3) | data formatting | bytes 2621440
Async XLA Ops:
  0.0 1.3 %copy-start = (f32[5,16,32,128]{3,2,1,0:T(8,128)S(1)}, f32[5,16,32,128]{3,2,1,0:T(8,128)}, u32[]{:S(2)}) copy-start(f32[5,16,32,128]{3,2,1,0:T(8,128)} %param.3) | copy-start | bytes 3932164
  1.3 0.9 %copy-start.1 = (f32[16,32,128]{2,1,0:T(8,128)S(1)}, f32[16,32,128]{2,1,0:T(8,128)}, u32[]{:S(2)}) copy-start(f32[16,32,128]{2,1,0:T(8,128)} %param.4) | copy-start | bytes 786436
  2.3 0.7 %copy-start.2 = (f32[5]{0:T(128)S(1)}, f32[5]{0:T(128)}, u32[]{:S(2)}) copy-start(f32[5]{0:T(128)} %spread.1) | copy-start | bytes 64

commit v2 on v1

--- a/solution.py
+++ b/solution.py
@@ -10,29 +10,30 @@
 PEERS = 16
 ROWS = NX * NY
 XM, XR, XV, YM, YR, YV = range(6)
-SHARE = {XM: 40, XR: 24, XV: 24, YM: 24, YR: 16, YV: 16}
-
-
-def ring(step, size):
-    return min(step, size - step)
-
-
-X_STEPS = sorted(
-    [(a, b) for a in range(4) for b in range(4) if (a, b) != (0, 0)],
-    key=lambda s: -(ring(s[0], 4) + ring(s[1], 4)),
+MESSAGES = {
+    XM: ("gx", 0, 0, 40),
+    XR: ("gx", 0, 40, 14),
+    XV: ("gx", 1, 0, 20),
+    YM: ("gy", 2, 0, 17),
+    YR: ("gy", 3, 0, 10),
+    YV: ("gy", 4, 0, 10),
+}
+SHARE = (56, 24, 24, 16, 16)
+
+X_STEPS = (
+    (2, 2), (2, 1), (1, 2), (2, 3), (3, 2), (1, 1), (1, 3), (3, 1),
+    (3, 3), (0, 2), (2, 0), (0, 1), (1, 0), (0, 3), (3, 0),
 )
-Y_STEPS = sorted(
-    [(a, b) for a in range(8) for b in range(2) if (a, b) != (0, 0)],
-    key=lambda s: -ring(s[0], 8),
+Y_STEPS = (
+    (4, 0), (4, 1), (3, 0), (3, 1), (5, 0), (5, 1), (2, 0), (2, 1),
+    (6, 0), (6, 1), (1, 0), (1, 1), (7, 0), (7, 1), (0, 1),
 )
 
 
 def partners(axis, gx, gy):
     if axis == "gx":
-        a, b = gx // 4, gx % 4
-        return [(((a + i) % 4) * 4 + (b + j) % 4, gy) for i, j in X_STEPS]
-    a, b = gy // 2, gy % 2
-    return [(gx, ((a + i) % 8) * 2 + (b + j) % 2) for i, j in Y_STEPS]
+        return [(((gx + 4 * i) & 12) + ((gx + j) & 3), gy) for i, j in X_STEPS]
+    return [(gx, ((gy + 2 * i) & 14) + ((gy + j) & 1)) for i, j in Y_STEPS]
 
 
 def rows(start, count):
@@ -85,12 +86,12 @@
 def kernel(
     fields_hbm, level_hbm, spread, out,
     field, level, visc, xg, xh, xq, xa, xb, xp, half, yg, yh, yq, ya, yb, yp,
-    s_xm, s_xr, s_xv, s_ym, s_yr, s_yv, r_xm, r_xr, r_xv, r_ym, r_yr, r_yv,
+    s_x, s_xv, s_ym, s_yr, s_yv, r_x, r_xv, r_ym, r_yr, r_yv,
     chain_p, chain_h, send_sem, recv_sem, in_sem,
 ):
     gx, gy = lax.axis_index("gx"), lax.axis_index("gy")
-    sends = (s_xm, s_xr, s_xv, s_ym, s_yr, s_yv)
-    recvs = (r_xm, r_xr, r_xv, r_ym, r_yr, r_yv)
+    sends = (s_x, s_xv, s_ym, s_yr, s_yv)
+    recvs = (r_x, r_xv, r_ym, r_yr, r_yv)
     everyone = partners("gx", gx, gy) + partners("gy", gx, gy)
 
     barrier = pltpu.get_barrier_semaphore()
@@ -101,30 +102,31 @@
     level_in.start()
     fields_in.start()
 
-    def axis_of(what):
-        return "gx" if what in (XM, XR, XV) else "gy"
-
     def send(what):
-        axis, size = axis_of(what), SHARE[what]
+        axis, buffer, first, count = MESSAGES[what]
+        size = SHARE[buffer]
         me = gx if axis == "gx" else gy
         for device in partners(axis, gx, gy):
             peer = device[0] if axis == "gx" else device[1]
             pltpu.make_async_remote_copy(
-                src_ref=sends[what].at[rows(pl.multiple_of(peer * size, 8), size)],
-                dst_ref=recvs[what].at[rows(pl.multiple_of(me * size, 8), size)],
+                src_ref=sends[buffer].at[rows(pl.multiple_of(peer * size, 8) + first, count)],
+                dst_ref=recvs[buffer].at[rows(pl.multiple_of(me * size, 8) + first, count)],
                 send_sem=send_sem.at[what],
                 recv_sem=recv_sem.at[what],
                 device_id=device,
                 device_id_type=MESH,
             ).start()
-        mine = rows(pl.multiple_of(me * size, 8), size)
-        recvs[what][mine] = sends[what][mine]
+
+    def keep(buffer, me):
+        mine = rows(pl.multiple_of(me * SHARE[buffer], 8), SHARE[buffer])
+        recvs[buffer][mine] = sends[buffer][mine]
 
     def total(what):
-        part = rows(0, (PEERS - 1) * SHARE[what])
+        axis, buffer, first, count = MESSAGES[what]
+        part = rows(0, (PEERS - 1) * count)
         return pltpu.make_async_remote_copy(
-            src_ref=sends[what].at[part],
-            dst_ref=recvs[what].at[part],
+            src_ref=sends[buffer].at[part],
+            dst_ref=recvs[buffer].at[part],
             send_sem=send_sem.at[what],
             recv_sem=recv_sem.at[what],
             device_id=everyone[0],
@@ -135,13 +137,19 @@
     zero = jnp.zeros((16, LANES), jnp.float32)
     one = jnp.ones((16, LANES), jnp.float32)
 
-    for ref, size, used in ((s_xm, 40, 34), (s_xr, 24, 20), (s_xv, 24, 20)):
-        for row in range(used, size):
+    for ref, size, unused in (
+        (s_x, 56, (54, 55)),
+        (s_xv, 24, (20, 21, 22, 23)),
+        (s_ym, 24, tuple(range(17, 24))),
+        (s_yr, 16, tuple(range(10, 16))),
+        (s_yv, 16, tuple(range(10, 16))),
+    ):
+        for row in unused:
             ref[pl.ds(row, 16, stride=size)] = zero
-    for ref, size, spare in ((s_ym, 24, (6, 7, 14, 15, 21, 22, 23)), (s_yr, 16, (5, 6, 7, 13, 14, 15))):
-        for row in spare:
+    for ref, size, unused in ((r_x, 56, (54, 55)), (r_ym, 24, tuple(range(17, 24))), (r_yr, 16, tuple(range(10, 16)))):
+        for row in unused:
             ref[pl.ds(row, 16, stride=size)] = zero
-    r_xr[rows(PEERS * SHARE[XR], 8)] = zero[:8]
+    r_x[rows(PEERS * 56, 8)] = zero[:8]
 
     level_in.wait()
 
@@ -195,16 +203,17 @@
         for f in range(FIELDS):
             for v, value in enumerate((first[f], mass[f], edge[f])):
                 base = v * 8 + 2 * f + s if f < 4 else 24 + 2 * v + s
-                s_xm[pl.ds(base, 16, stride=40)] = value
+                s_x[pl.ds(base, 16, stride=56)] = value
             for v, value in enumerate((first_right[f], right[f])):
-                base = v * 8 + 2 * f + s if f < 4 else 16 + 2 * v + s
-                s_xr[pl.ds(base, 16, stride=24)] = value
-        s_xm[pl.ds(30 + s, 16, stride=40)] = nu0
-        s_xm[pl.ds(32 + s, 16, stride=40)] = nu
+                base = 34 + v * 8 + 2 * f + s if f < 4 else 50 + 2 * v + s
+                s_x[pl.ds(base, 16, stride=56)] = value
+        s_x[pl.ds(30 + s, 16, stride=56)] = nu0
+        s_x[pl.ds(32 + s, 16, stride=56)] = nu
 
     pl.semaphore_wait(barrier, len(everyone))
     send(XM)
     send(XR)
+    keep(0, gx)
 
     def y_visc(j):
         return visc[pl.ds(j, 16, stride=NY)]
@@ -236,10 +245,11 @@
     nu, edge, mass, first = lax.fori_loop(1, NY - 1, forward, start)
     for f in range(FIELDS):
         for v, value in enumerate((first[f], mass[f], edge[f])):
-            s_ym[pl.ds(v * 8 + f, 16, stride=24)] = value
-    s_ym[pl.ds(5, 16, stride=24)] = nu0
-    s_ym[pl.ds(13, 16, stride=24)] = nu
+            s_ym[pl.ds(v * 5 + f, 16, stride=24)] = value
+    s_ym[pl.ds(15, 16, stride=24)] = nu0
+    s_ym[pl.ds(16, 16, stride=24)] = nu
     send(YM)
+    keep(2, gy)
 
     for s in range(2):
         for f in range(FIELDS):
@@ -272,16 +282,16 @@
 
     def x_mass(j):
         v = j % 2
-        return pack(r_xm, j // 2, 40, 8 * v, 24 + 2 * v)
+        return pack(r_x, j // 2, 56, 8 * v, 24 + 2 * v)
 
     def x_end_visc(k, v):
-        base = k * 40 + 30 + 2 * v
-        return jnp.where(odd, r_xm[rows(base + 1, 1)], r_xm[rows(base, 1)])
+        base = k * 56 + 30 + 2 * v
+        return jnp.where(odd, r_x[rows(base + 1, 1)], r_x[rows(base, 1)])
 
     def x_link(j):
         k = j // 2
         if j % 2 == 0:
-            return pack(r_xm, k, 40, 16, 28)
+            return pack(r_x, k, 56, 16, 28)
         return rate_x * (x_end_visc(k, 1) + x_end_visc(k + 1, 0))
 
     total(XM).wait_recv()
@@ -289,12 +299,13 @@
         x_mass, x_link, 2.0 * rate_x * x_end_visc(0, 0), 2.0 * rate_x * x_end_visc(PEERS - 1, 1), PEERS
     )
     total(XR).wait_recv()
-    solved = chain_solve(parts, lambda j: pack(r_xr, j // 2, 24, 8 * (j % 2), 16 + 2 * (j % 2)), PEERS)
+    solved = chain_solve(parts, lambda j: pack(r_x, j // 2, 56, 34 + 8 * (j % 2), 50 + 2 * (j % 2)), PEERS)
     for k in range(PEERS):
         for v in range(2):
             s_xv[rows(k * 24 + 8 * v, 8)] = solved[2 * k + v][:8]
             s_xv[rows(k * 24 + 16 + 2 * v, 2)] = solved[2 * k + v][8:10]
     send(XV)
+    keep(1, gx)
 
     def natural(f, j):
         return pl.ds(f * ROWS + j, 16, stride=NY)
@@ -324,17 +335,17 @@
         rate_y = jnp.where(line == f, rate[f], rate_y)
 
     def y_end_visc(k, v):
-        return r_ym[rows(k * 24 + 5 + 8 * v, 1)]
+        return r_ym[rows(k * 24 + 15 + v, 1)]
 
     def y_link(j):
         k = j // 2
         if j % 2 == 0:
-            return r_ym[rows(k * 24 + 16, 8)]
+            return r_ym[rows(k * 24 + 10, 8)]
         return rate_y * (y_end_visc(k, 1) + y_end_visc(k + 1, 0))
 
     total(YM).wait_recv()
     low, high, middle = chain_matrix(
-        lambda j: r_ym[rows((j // 2) * 24 + 8 * (j % 2), 8)],
+        lambda j: r_ym[rows((j // 2) * 24 + 5 * (j % 2), 8)],
         y_link,
         2.0 * rate_y * y_end_visc(0, 0),
         2.0 * rate_y * y_end_visc(PEERS - 1, 1),
@@ -360,11 +371,12 @@
             value = xp[at] + xa[at] * low_end + xb[at] * high_end
             half[at] = value
             s_yr[rows(i * 16 + f, 1)] = jnp.sum(ya[at] * value, axis=0, keepdims=True)
-            s_yr[rows(i * 16 + 8 + f, 1)] = jnp.sum(yb[at] * value, axis=0, keepdims=True)
+            s_yr[rows(i * 16 + 5 + f, 1)] = jnp.sum(yb[at] * value, axis=0, keepdims=True)
             return carry
 
-        lax.fori_loop(0, NX, finish_x, 0)
+        lax.fori_loop(0, NX, finish_x, 0, unroll=8)
     send(YR)
+    keep(3, gy)
 
     def forward(j, right):
         new = []
@@ -396,22 +408,23 @@
         ]
         for side in range(2)
     ) + (middle,)
-    solved = chain_solve(parts, lambda j: r_yr[rows((j // 2) * 16 + 8 * (j % 2), 8)], PEERS)
+    solved = chain_solve(parts, lambda j: r_yr[rows((j // 2) * 16 + 5 * (j % 2), 8)], PEERS)
     for k in range(PEERS):
         for v in range(2):
-            s_yv[rows(k * 16 + 8 * v, 8)] = solved[2 * k + v]
+            s_yv[rows(k * 16 + 5 * v, 5)] = solved[2 * k + v][:5]
     send(YV)
+    keep(4, gy)
 
     total(YV).wait_recv()
 
     def finish_y(i, carry):
         for f in range(FIELDS):
             at = rows(pl.multiple_of(f * ROWS + i * NY, NY), NY)
-            low_end, high_end = r_yv[rows(i * 16 + f, 1)], r_yv[rows(i * 16 + 8 + f, 1)]
+            low_end, high_end = r_yv[rows(i * 16 + f, 1)], r_yv[rows(i * 16 + 5 + f, 1)]
             out[at] = yp[at] + ya[at] * low_end + yb[at] * high_end
         return carry
 
-    lax.fori_loop(0, NX, finish_y, 0)
+    lax.fori_loop(0, NX, finish_y, 0, unroll=2)
     for what in range(6):
         total(what).wait_send()
 
@@ -421,11 +434,11 @@
         return pltpu.VMEM((count, LANES), jnp.float32)
 
     whole = buffer(FIELDS * ROWS)
-    messages = [buffer(PEERS * SHARE[what]) for what in range(6)]
-    arrivals = [buffer(PEERS * SHARE[what] + 8) for what in range(6)]
+    messages = [buffer(PEERS * size) for size in SHARE]
+    arrivals = [buffer(PEERS * size + 8) for size in SHARE]
     solved = pl.pallas_call(
         kernel,
-        out_shape=jax.ShapeDtypeStruct((FIELDS * ROWS, LANES), jnp.float32),
+        out_shape=pltpu.VMEM((FIELDS * ROWS, LANES), jnp.float32),
         in_specs=[
             pl.BlockSpec(memory_space=pl.ANY),
             pl.BlockSpec(memory_space=pl.ANY),
@@ -444,7 +457,7 @@
             pltpu.SemaphoreType.DMA((2,)),
         ],
         compiler_params=pltpu.CompilerParams(
-            collective_id=0, has_side_effects=True, vmem_limit_bytes=48 * 1024 * 1024
+            collective_id=0, has_side_effects=True, vmem_limit_bytes=60 * 1024 * 1024
         ),
     )(
         conserved_states.reshape(FIELDS * ROWS, LANES),

time: 40.9 us -> 35.4 us (0.87)
  local copies, waits for them, and re-layouts: 3.98 us -> 1.06 us
  Pallas kernels: 36.8 us -> 34.2 us
    unnamed x7 -> x1, local copies, waits for them, and re-layouts: 3.98 us -> 1.06 us
    pallas_call x1, Pallas kernels: 36.8 us -> 34.2 us  [shards(): pl.pallas_call(kernel, out_shape=pltpu.VMEM((FIELDS * ROWS, LANES), jnp.f...]
where the time goes in v2:
time: 35.4 us; the launch traced here: 35.3 us
  Pallas kernels  34.2 us (97%)
  local copies, waits for them, and re-layouts  1.06 us (3%)
    pallas_call x1, Pallas kernels, shards(): pl.pallas_call(kernel, out_shape=pltpu.VMEM((FIELDS * ROWS, LANES), jnp.f...  34.2 us
    unnamed x1, local copies, waits for them, and re-layouts  1.06 us

profile of v2, /device:TPU:1, one launch (start us, length us, event | category | flops | bytes accessed | tf_op | source)
XLA Modules:
  0.0 35.3 jit_solution(8844138206833523170)
XLA Ops:
  0.0 34.2 %shard_map.37 = f32[2560,128]{1,0:T(8,128)S(1)} custom-call(f32[2560,128]{1,0:T(8,128)} %bitcast.4, f32[512,128]{1,0:T(8,128)} %bitcast.5, f32[5]{0:T(128)} %spread.1), custom_call_target="tpu_custom_call" | custom-call | tf_op jit(solution)/shard_map/pallas_call | solution.py:439
  34.2 1.1 %copy.5 = f32[5,16,32,128]{3,2,1,0:T(8,128)} copy(f32[5,16,32,128]{3,2,1,0:T(8,128)S(1)} %bitcast.3) | data formatting | bytes 2621440

commit v3 on v1

v3 whole, which is shorter than its diff:
```python
import jax
import jax.numpy as jnp
from jax import lax
from jax.experimental import pallas as pl
from jax.experimental.pallas import tpu as pltpu
from jax.sharding import PartitionSpec as P

MESH = pl.DeviceIdType.MESH
FIELDS, NX, NY, LANES = 5, 16, 32, 128
PEERS = 16
ROWS = NX * NY
GROUPS = ((0, 1, 2), (3, 4))


def message_table():
    table = {"ym": ("gy", 3 * FIELDS + 2, 24)}
    for g, group in enumerate(GROUPS):
        n = len(group)
        for name, axis, count in (
            ("xo", "gx", 10 * n + (4 if g == 0 else 0)),
            ("xv", "gx", 4 * n),
            ("yr", "gy", 2 * n),
            ("yv", "gy", 2 * n),
        ):
            table[name, g] = (axis, count, -(-count // 8) * 8)
    return table


MESSAGES = message_table()
ORDER = {what: k for k, what in enumerate(MESSAGES)}

X_STEPS = (
    (2, 2), (2, 1), (1, 2), (2, 3), (3, 2), (1, 1), (1, 3), (3, 1),
    (3, 3), (0, 2), (2, 0), (0, 1), (1, 0), (0, 3), (3, 0),
)
Y_STEPS = (
    (4, 0), (4, 1), (3, 0), (3, 1), (5, 0), (5, 1), (2, 0), (2, 1),
    (6, 0), (6, 1), (1, 0), (1, 1), (7, 0), (7, 1), (0, 1),
)


def partners(axis, gx, gy):
    if axis == "gx":
        return [(((gx + 4 * i) & 12) + ((gx + j) & 3), gy) for i, j in X_STEPS]
    return [(gx, ((gy + 2 * i) & 14) + ((gy + j) & 1)) for i, j in Y_STEPS]


def rows(start, count):
    return pl.ds(start, count)


def chain_matrix(mass, link, wall_low, wall_high, half):
    sides = []
    last = 2 * half - 1
    for low in (True, False):
        at = (lambda j: j) if low else (lambda j: last - j)
        edge = (lambda j: link(j)) if low else (lambda j: link(last - j - 1))
        m = mass(at(0)) + (wall_low if low else wall_high)
        steps = []
        for j in range(half - 1):
            e = edge(j)
            p = 1.0 / (m + e)
            h = e * p
            steps.append((p, h))
            m = mass(at(j + 1)) + h * m
        sides.append((steps, m))
    w = link(half - 1)
    m_low, m_high = sides[0][1], sides[1][1]
    inverse = 1.0 / (m_low * m_high + w * (m_low + m_high))
    middle = ((m_high + w) * inverse, w * inverse, (m_low + w) * inverse)
    return sides[0][0], sides[1][0], middle


def chain_solve(parts, right, half):
    low, high, (a, b, c) = parts
    last = 2 * half - 1
    ends, kept = [], []
    for steps, at in ((low, lambda j: j), (high, lambda j: last - j)):
        r = right(at(0))
        q = []
        for j, (p, h) in enumerate(steps):
            q.append(p * r)
            r = right(at(j + 1)) + h * r
        ends.append(r)
        kept.append(q)
    values = [None] * (2 * half)
    values[half - 1] = a * ends[0] + b * ends[1]
    values[half] = b * ends[0] + c * ends[1]
    for j in range(half - 2, -1, -1):
        values[j] = kept[0][j] + low[j][1] * values[j + 1]
        values[last - j] = kept[1][j] + high[j][1] * values[last - j - 1]
    return values


def kernel(
    fields_hbm, level_hbm, spread, out,
    field, level, visc, xg, xh, xq, xa, xb, xp, half, yg, yh, yq, ya, yb, yp,
    *rest,
):
    gx, gy = lax.axis_index("gx"), lax.axis_index("gy")
    count = len(MESSAGES)
    sends = dict(zip(MESSAGES, rest[:count]))
    recvs = dict(zip(MESSAGES, rest[count : 2 * count]))
    chain_p, chain_h, send_sem, recv_sem, in_sem = rest[2 * count :]
    everyone = partners("gx", gx, gy) + partners("gy", gx, gy)

    barrier = pltpu.get_barrier_semaphore()
    for device in everyone:
        pl.semaphore_signal(barrier, inc=1, device_id=device, device_id_type=MESH)
    level_in = pltpu.make_async_copy(level_hbm, level, in_sem.at[0])
    fields_in = pltpu.make_async_copy(fields_hbm, field, in_sem.at[1])
    level_in.start()
    fields_in.start()

    def send(what):
        axis, count, size = MESSAGES[what]
        me = gx if axis == "gx" else gy
        for device in partners(axis, gx, gy):
            peer = device[0] if axis == "gx" else device[1]
            pltpu.make_async_remote_copy(
                src_ref=sends[what].at[rows(pl.multiple_of(peer * size, 8), count)],
                dst_ref=recvs[what].at[rows(pl.multiple_of(me * size, 8), count)],
                send_sem=send_sem.at[ORDER[what]],
                recv_sem=recv_sem.at[ORDER[what]],
                device_id=device,
                device_id_type=MESH,
            ).start()

    def keep(what):
        axis, count, size = MESSAGES[what]
        mine = rows(pl.multiple_of((gx if axis == "gx" else gy) * size, 8), size)
        recvs[what][mine] = sends[what][mine]

    def total(what):
        axis, count, size = MESSAGES[what]
        part = rows(0, (PEERS - 1) * count)
        return pltpu.make_async_remote_copy(
            src_ref=sends[what].at[part],
            dst_ref=recvs[what].at[part],
            send_sem=send_sem.at[ORDER[what]],
            recv_sem=recv_sem.at[ORDER[what]],
            device_id=everyone[0],
            device_id_type=MESH,
        )

    def share(what, row):
        return pl.ds(row, PEERS, stride=MESSAGES[what][2])

    def peer_rows(what, k, row, count=8):
        return rows(k * MESSAGES[what][2] + row, count)

    rate = [2500.0 * spread[f] for f in range(FIELDS)]
    zero = jnp.zeros((16, LANES), jnp.float32)
    one = jnp.ones((16, LANES), jnp.float32)

    for what, (axis, used, size) in MESSAGES.items():
        for row in range(used, size):
            sends[what][share(what, row)] = zero
            recvs[what][share(what, row)] = zero
        recvs[what][rows(PEERS * size, 8)] = zero[:8]

    level_in.wait()

    def power(t, carry):
        at = rows(pl.multiple_of(t * 64, 64), 64)
        visc[at] = jnp.exp(0.7 * jnp.log(level[at]))
        return carry

    lax.fori_loop(0, ROWS // 64, power, 0)
    fields_in.wait()

    def x_row(f, i, s):
        return rows(pl.multiple_of(f * ROWS + i * NY + s * 16, 16), 16)

    def x_visc(i, s):
        return visc[rows(pl.multiple_of(i * NY + s * 16, 16), 16)]

    for s in range(2):
        nu0, nu1 = x_visc(0, s), x_visc(1, s)
        start = (
            nu1,
            tuple(rate[f] * (nu0 + nu1) for f in range(FIELDS)),
            (one,) * FIELDS,
            (one,) * FIELDS,
            tuple(field[x_row(f, 1, s)] for f in range(FIELDS)),
            tuple(field[x_row(f, 0, s)] for f in range(FIELDS)),
        )

        def forward(i, state, s=s):
            nu, edge, mass, first, right, first_right = state
            nu_next = x_visc(i + 1, s)
            face = nu + nu_next
            out_state = ([], [], [], [], [])
            for f in range(FIELDS):
                e, m, r = edge[f], mass[f], right[f]
                w = rate[f] * face
                p = 1.0 / (e + w + m)
                g, h = e * p, w * p
                at = x_row(f, i, s)
                xg[at] = g
                xh[at] = h
                xq[at] = p * r
                for box, item in zip(
                    out_state,
                    (g * w, 1.0 + h * m, first[f] + g * m, field[x_row(f, i + 1, s)] + h * r, first_right[f] + g * r),
                ):
                    box.append(item)
            return (nu_next,) + tuple(tuple(box) for box in out_state)

        nu, edge, mass, first, right, first_right = lax.fori_loop(1, NX - 1, forward, start)
        for g, group in enumerate(GROUPS):
            what, n = ("xo", g), 2 * len(group)
            for place, f in enumerate(group):
                for v, value in enumerate((first[f], mass[f], edge[f], first_right[f], right[f])):
                    sends[what][share(what, v * n + 2 * place + s)] = value
        what, n = ("xo", 0), 10 * len(GROUPS[0])
        sends[what][share(what, n + s)] = nu0
        sends[what][share(what, n + 2 + s)] = nu

    pl.semaphore_wait(barrier, len(everyone))
    for g in range(len(GROUPS)):
        send(("xo", g))
    for g in range(len(GROUPS)):
        keep(("xo", g))

    def y_visc(j):
        return visc[pl.ds(j, 16, stride=NY)]

    def y_row(f, j):
        return rows(pl.multiple_of((f * NY + j) * 16, 16), 16)

    nu0, nu1 = y_visc(0), y_visc(1)
    start = (nu1, tuple(rate[f] * (nu0 + nu1) for f in range(FIELDS)), (one,) * FIELDS, (one,) * FIELDS)

    def forward(j, state):
        nu, edge, mass, first = state
        nu_next = y_visc(j + 1)
        face = nu + nu_next
        out_state = ([], [], [])
        for f in range(FIELDS):
            e, m = edge[f], mass[f]
            w = rate[f] * face
            p = 1.0 / (e + w + m)
            g, h = e * p, w * p
            at = y_row(f, j)
            yg[at] = g
            yh[at] = h
            yq[at] = p
            for box, item in zip(out_state, (g * w, 1.0 + h * m, first[f] + g * m)):
                box.append(item)
        return (nu_next,) + tuple(tuple(box) for box in out_state)

    nu, edge, mass, first = lax.fori_loop(1, NY - 1, forward, start)
    at = 0
    y_at = []
    for group in GROUPS:
        y_at.append(at)
        for v, values in enumerate((first, mass, edge)):
            for f in group:
                sends["ym"][share("ym", at)] = values[f]
                at += 1
    sends["ym"][share("ym", at)] = nu0
    sends["ym"][share("ym", at + 1)] = nu
    send("ym")
    keep("ym")

    for s in range(2):
        for f in range(FIELDS):
            for i, ends in ((0, (one, zero)), (NX - 1, (zero, one))):
                at = x_row(f, i, s)
                xa[at], xb[at], xp[at] = ends[0], ends[1], zero

        def backward(k, state, s=s):
            i = NX - 2 - k
            new = []
            for f in range(FIELDS):
                a, b, p = state[f]
                at = x_row(f, i, s)
                h = xh[at]
                a, b, p = xg[at] + h * a, h * b, xq[at] + h * p
                xa[at], xb[at], xp[at] = a, b, p
                new.append((a, b, p))
            return tuple(new)

        lax.fori_loop(0, NX - 2, backward, ((zero, one, zero),) * FIELDS)

    line = lax.broadcasted_iota(jnp.int32, (8, LANES), 0)

    def rates(group, each):
        value = jnp.full((8, LANES), rate[group[-1]], jnp.float32)
        for place, f in enumerate(group[:-1]):
            value = jnp.where(line // each == place, rate[f], value)
        return value

    for g, group in enumerate(GROUPS):
        what, n = ("xo", g), 2 * len(group)
        rate_x = rates(group, 2)

        def end_visc(k, v):
            base = 10 * len(GROUPS[0]) + 2 * v
            low, high = (recvs["xo", 0][peer_rows(("xo", 0), k, base + s, 1)] for s in range(2))
            return jnp.where(line % 2 == 1, high, low)

        def link(j):
            if j % 2 == 0:
                return recvs[what][peer_rows(what, j // 2, 2 * n)]
            return rate_x * (end_visc(j // 2, 1) + end_visc(j // 2 + 1, 0))

        total(what).wait_recv()
        parts = chain_matrix(
            lambda j: recvs[what][peer_rows(what, j // 2, n * (j % 2))],
            link,
            2.0 * rate_x * end_visc(0, 0),
            2.0 * rate_x * end_visc(PEERS - 1, 1),
            PEERS,
        )
        solved = chain_solve(parts, lambda j: recvs[what][peer_rows(what, j // 2, n * (3 + j % 2))], PEERS)
        back = ("xv", g)
        for k in range(PEERS):
            for v in range(2):
                sends[back][peer_rows(back, k, n * v, n)] = solved[2 * k + v][:n]
        send(back)
        keep(back)

    def natural(f, j):
        return pl.ds(f * ROWS + j, 16, stride=NY)

    for f in range(FIELDS):
        for j, ends in ((0, (one, zero)), (NY - 1, (zero, one))):
            at = natural(f, j)
            ya[at], yb[at], yp[at] = ends[0], ends[1], zero

    def backward(k, state):
        j = NY - 2 - k
        new = []
        for f in range(FIELDS):
            a, b = state[f]
            at = y_row(f, j)
            h = yh[at]
            a, b = yg[at] + h * a, h * b
            ya[natural(f, j)], yb[natural(f, j)] = a, b
            new.append((a, b))
        return tuple(new)

    lax.fori_loop(0, NY - 2, backward, ((zero, one),) * FIELDS)

    total("ym").wait_recv()
    middles = []
    for g, group in enumerate(GROUPS):
        n = len(group)
        rate_y = rates(group, 1)

        def end_visc(k, v):
            return recvs["ym"][peer_rows("ym", k, 3 * FIELDS + v, 1)]

        def link(j):
            if j % 2 == 0:
                return recvs["ym"][peer_rows("ym", j // 2, y_at[g] + 2 * n)]
            return rate_y * (end_visc(j // 2, 1) + end_visc(j // 2 + 1, 0))

        low, high, middle = chain_matrix(
            lambda j: recvs["ym"][peer_rows("ym", j // 2, y_at[g] + n * (j % 2))],
            link,
            2.0 * rate_y * end_visc(0, 0),
            2.0 * rate_y * end_visc(PEERS - 1, 1),
            PEERS,
        )
        middles.append(middle)
        for side, steps in enumerate((low, high)):
            for j, (p, h) in enumerate(steps):
                at = rows(((2 * g + side) * PEERS + j) * 8, 8)
                chain_p[at] = p
                chain_h[at] = h

    for g, group in enumerate(GROUPS):
        what, back, n = ("yr", g), ("xv", g), len(group)
        total(back).wait_recv()
        for place, f in enumerate(group):
            low_end, high_end = (
                jnp.concatenate(
                    [recvs[back][share(back, 2 * n * v + 2 * place + s)] for s in range(2)], axis=0
                )
                for v in range(2)
            )

            def finish_x(i, carry, f=f, place=place, low_end=low_end, high_end=high_end):
                at = rows(pl.multiple_of(f * ROWS + i * NY, NY), NY)
                value = xp[at] + xa[at] * low_end + xb[at] * high_end
                half[at] = value
                low = jnp.sum(ya[at] * value, axis=0, keepdims=True)
                high = jnp.sum(yb[at] * value, axis=0, keepdims=True)
                sends[what][peer_rows(what, i, place, 1)] = low
                sends[what][peer_rows(what, i, n + place, 1)] = high
                return carry

            lax.fori_loop(0, NX, finish_x, 0, unroll=8)
        send(what)
        keep(what)

    def forward(j, right):
        new = []
        for f in range(FIELDS):
            at = y_row(f, j)
            yg[at] = yq[at] * right[f]
            new.append(half[natural(f, j + 1)] + yh[at] * right[f])
        return tuple(new)

    lax.fori_loop(1, NY - 1, forward, tuple(half[natural(f, 1)] for f in range(FIELDS)))

    def backward(k, state):
        j = NY - 2 - k
        new = []
        for f in range(FIELDS):
            at = y_row(f, j)
            p = yg[at] + yh[at] * state[f]
            yp[natural(f, j)] = p
            new.append(p)
        return tuple(new)

    lax.fori_loop(0, NY - 2, backward, (zero,) * FIELDS)

    for g, group in enumerate(GROUPS):
        what, back, n = ("yr", g), ("yv", g), len(group)
        parts = []
        for side in range(2):
            at = [rows(((2 * g + side) * PEERS + j) * 8, 8) for j in range(PEERS - 1)]
            parts.append([(chain_p[place], chain_h[place]) for place in at])
        total(what).wait_recv()
        solved = chain_solve(
            (*parts, middles[g]), lambda j: recvs[what][peer_rows(what, j // 2, n * (j % 2))], PEERS
        )
        for k in range(PEERS):
            for v in range(2):
                sends[back][peer_rows(back, k, n * v, n)] = solved[2 * k + v][:n]
        send(back)
        keep(back)

    for g, group in enumerate(GROUPS):
        back, n = ("yv", g), len(group)
        total(back).wait_recv()

        def finish_y(i, carry):
            for place, f in enumerate(group):
                at = rows(pl.multiple_of(f * ROWS + i * NY, NY), NY)
                low_end = recvs[back][peer_rows(back, i, place, 1)]
                high_end = recvs[back][peer_rows(back, i, n + place, 1)]
                out[at] = yp[at] + ya[at] * low_end + yb[at] * high_end
            return carry

        lax.fori_loop(0, NX, finish_y, 0, unroll=2)
    for what in MESSAGES:
        total(what).wait_send()


def shards(conserved_states, thermal_level, spread_factors):
    def buffer(count):
        return pltpu.VMEM((count, LANES), jnp.float32)

    whole = buffer(FIELDS * ROWS)
    messages = [buffer(PEERS * size) for axis, count, size in MESSAGES.values()]
    arrivals = [buffer(PEERS * size + 8) for axis, count, size in MESSAGES.values()]
    solved = pl.pallas_call(
        kernel,
        out_shape=pltpu.VMEM((FIELDS * ROWS, LANES), jnp.float32),
        in_specs=[
            pl.BlockSpec(memory_space=pl.ANY),
            pl.BlockSpec(memory_space=pl.ANY),
            pl.BlockSpec(memory_space=pltpu.SMEM),
        ],
        out_specs=pl.BlockSpec(memory_space=pltpu.VMEM),
        scratch_shapes=[whole, buffer(ROWS), buffer(ROWS)]
        + [whole] * 13
        + messages
        + arrivals
        + [
            buffer(2 * len(GROUPS) * PEERS * 8),
            buffer(2 * len(GROUPS) * PEERS * 8),
            pltpu.SemaphoreType.DMA((len(MESSAGES),)),
            pltpu.SemaphoreType.DMA((len(MESSAGES),)),
            pltpu.SemaphoreType.DMA((2,)),
        ],
        compiler_params=pltpu.CompilerParams(
            collective_id=0, has_side_effects=True, vmem_limit_bytes=60 * 1024 * 1024
        ),
    )(
        conserved_states.reshape(FIELDS * ROWS, LANES),
        thermal_level.reshape(ROWS, LANES),
        spread_factors,
    )
    return solved.reshape(conserved_states.shape)


def solution(mesh):
    return jax.shard_map(
        shards,
        mesh=mesh,
        in_specs=(P(None, "gx", "gy", None), P("gx", "gy", None), P()),
        out_specs=P(None, "gx", "gy", None),
        check_vma=False,
    )
```

time: 40.9 us -> 34.8 us (0.85)
  Pallas kernels: 36.8 us -> 33.6 us
  local copies, waits for them, and re-layouts: 3.98 us -> 1.06 us
    pallas_call x1, Pallas kernels: 36.8 us -> 33.6 us  [shards(): pl.pallas_call(kernel, out_shape=pltpu.VMEM((FIELDS * ROWS, LANES), jnp.f...]
    unnamed x7 -> x1, local copies, waits for them, and re-layouts: 3.98 us -> 1.06 us
where the time goes in v3:
time: 34.8 us; the launch traced here: 34.7 us
  Pallas kernels  33.6 us (97%)
  local copies, waits for them, and re-layouts  1.06 us (3%)
    pallas_call x1, Pallas kernels, shards(): pl.pallas_call(kernel, out_shape=pltpu.VMEM((FIELDS * ROWS, LANES), jnp.f...  33.6 us
    unnamed x1, local copies, waits for them, and re-layouts  1.06 us

profile of v3, /device:TPU:1, one launch (start us, length us, event | category | flops | bytes accessed | tf_op | source)
XLA Modules:
  0.0 34.7 jit_solution(5578050093835854441)
XLA Ops:
  0.0 33.6 %shard_map.37 = f32[2560,128]{1,0:T(8,128)S(1)} custom-call(f32[2560,128]{1,0:T(8,128)} %bitcast.4, f32[512,128]{1,0:T(8,128)} %bitcast.5, f32[5]{0:T(128)} %spread.1), custom_call_target="tpu_custom_call" | custom-call | tf_op jit(solution)/shard_map/pallas_call | solution.py:462
  33.7 1.1 %copy.5 = f32[5,16,32,128]{3,2,1,0:T(8,128)} copy(f32[5,16,32,128]{3,2,1,0:T(8,128)S(1)} %bitcast.3) | data formatting | bytes 2621440

commit v4 on v3

--- a/solution.py
+++ b/solution.py
@@ -37,6 +37,19 @@
     (4, 0), (4, 1), (3, 0), (3, 1), (5, 0), (5, 1), (2, 0), (2, 1),
     (6, 0), (6, 1), (1, 0), (1, 1), (7, 0), (7, 1), (0, 1),
 )
+
+
+X_FIRST = tuple(range(16))
+Y_FIRST = (1, 3, 9, 5, 8, 2, 7, 11, 4, 10, 6, 13, 15, 12, 0, 14)
+
+
+def ring(step, size):
+    return min(step, size - step)
+
+
+def others(order, me):
+    place = sum(k * (me == at).astype(jnp.int32) for k, at in enumerate(order))
+    return [jnp.where(place > k, order[k], order[k + 1]) for k in range(len(order) - 1)]
 
 
 def partners(axis, gx, gy):
@@ -103,19 +116,24 @@
     recvs = dict(zip(MESSAGES, rest[count : 2 * count]))
     chain_p, chain_h, send_sem, recv_sem, in_sem = rest[2 * count :]
     everyone = partners("gx", gx, gy) + partners("gy", gx, gy)
+    hops = [ring(i, 4) + ring(j, 4) for i, j in X_STEPS] + [ring(i, 8) for i, j in Y_STEPS]
+    greeted = [everyone[k] for k in sorted(range(len(everyone)), key=lambda k: -hops[k])]
 
     barrier = pltpu.get_barrier_semaphore()
-    for device in everyone:
+    for device in greeted:
         pl.semaphore_signal(barrier, inc=1, device_id=device, device_id_type=MESH)
     level_in = pltpu.make_async_copy(level_hbm, level, in_sem.at[0])
     fields_in = pltpu.make_async_copy(fields_hbm, field, in_sem.at[1])
     level_in.start()
     fields_in.start()
 
-    def send(what):
+    x_order = [(peer, gy) for peer in others(X_FIRST, gx)]
+    y_order = [(gx, peer) for peer in others(Y_FIRST, gy)]
+
+    def send(what, devices=None):
         axis, count, size = MESSAGES[what]
         me = gx if axis == "gx" else gy
-        for device in partners(axis, gx, gy):
+        for device in devices or partners(axis, gx, gy):
             peer = device[0] if axis == "gx" else device[1]
             pltpu.make_async_remote_copy(
                 src_ref=sends[what].at[rows(pl.multiple_of(peer * size, 8), count)],
@@ -319,8 +337,10 @@
         for k in range(PEERS):
             for v in range(2):
                 sends[back][peer_rows(back, k, n * v, n)] = solved[2 * k + v][:n]
-        send(back)
+        send(back, x_order[:7])
         keep(back)
+    for g in range(len(GROUPS)):
+        send(("xv", g), x_order[7:])
 
     def natural(f, j):
         return pl.ds(f * ROWS + j, 16, stride=NY)
@@ -432,7 +452,7 @@
         for k in range(PEERS):
             for v in range(2):
                 sends[back][peer_rows(back, k, n * v, n)] = solved[2 * k + v][:n]
-        send(back)
+        send(back, y_order)
         keep(back)
 
     for g, group in enumerate(GROUPS):

time: 34.8 us -> 34.4 us (0.989)
  Pallas kernels: 33.6 us -> 33.2 us
    pallas_call x1, Pallas kernels: 33.6 us -> 33.2 us  [shards(): pl.pallas_call(kernel, out_shape=pltpu.VMEM((FIELDS * ROWS, LANES), jnp.f...]
where the time goes in v4:
time: 34.4 us; the launch traced here: 34.3 us
  Pallas kernels  33.2 us (97%)
  local copies, waits for them, and re-layouts  1.06 us (3%)
    pallas_call x1, Pallas kernels, shards(): pl.pallas_call(kernel, out_shape=pltpu.VMEM((FIELDS * ROWS, LANES), jnp.f...  33.2 us
    unnamed x1, local copies, waits for them, and re-layouts  1.06 us

profile of v4, /device:TPU:1, one launch (start us, length us, event | category | flops | bytes accessed | tf_op | source)
XLA Modules:
  0.0 34.3 jit_solution(12472129564179838611)
XLA Ops:
  0.0 33.2 %shard_map.37 = f32[2560,128]{1,0:T(8,128)S(1)} custom-call(f32[2560,128]{1,0:T(8,128)} %bitcast.4, f32[512,128]{1,0:T(8,128)} %bitcast.5, f32[5]{0:T(128)} %spread.1), custom_call_target="tpu_custom_call" | custom-call | tf_op jit(solution)/shard_map/pallas_call | solution.py:482
  33.2 1.1 %copy.5 = f32[5,16,32,128]{3,2,1,0:T(8,128)} copy(f32[5,16,32,128]{3,2,1,0:T(8,128)S(1)} %bitcast.3) | data formatting | bytes 2621440

commit v5 on v4

--- a/solution.py
+++ b/solution.py
@@ -62,59 +62,57 @@
     return pl.ds(start, count)
 
 
-def chain_matrix(mass, link, wall_low, wall_high, half):
-    sides = []
-    last = 2 * half - 1
-    for low in (True, False):
-        at = (lambda j: j) if low else (lambda j: last - j)
-        edge = (lambda j: link(j)) if low else (lambda j: link(last - j - 1))
-        m = mass(at(0)) + (wall_low if low else wall_high)
-        steps = []
-        for j in range(half - 1):
-            e = edge(j)
-            p = 1.0 / (m + e)
-            h = e * p
-            steps.append((p, h))
-            m = mass(at(j + 1)) + h * m
-        sides.append((steps, m))
-    w = link(half - 1)
-    m_low, m_high = sides[0][1], sides[1][1]
-    inverse = 1.0 / (m_low * m_high + w * (m_low + m_high))
-    middle = ((m_high + w) * inverse, w * inverse, (m_low + w) * inverse)
-    return sides[0][0], sides[1][0], middle
-
-
-def chain_solve(parts, right, half):
-    low, high, (a, b, c) = parts
-    last = 2 * half - 1
-    ends, kept = [], []
-    for steps, at in ((low, lambda j: j), (high, lambda j: last - j)):
-        r = right(at(0))
-        q = []
-        for j, (p, h) in enumerate(steps):
-            q.append(p * r)
-            r = right(at(j + 1)) + h * r
-        ends.append(r)
-        kept.append(q)
-    values = [None] * (2 * half)
-    values[half - 1] = a * ends[0] + b * ends[1]
-    values[half] = b * ends[0] + c * ends[1]
-    for j in range(half - 2, -1, -1):
-        values[j] = kept[0][j] + low[j][1] * values[j + 1]
-        values[last - j] = kept[1][j] + high[j][1] * values[last - j - 1]
+def chain_matrix(mass, link, wall_low, wall_high, count):
+    masses = [mass(j) for j in range(count)]
+    links = [link(j) for j in range(count - 1)]
+    masses[0] += wall_low
+    masses[-1] += wall_high
+    nodes, steps = list(range(count)), []
+    while len(nodes) > 1:
+        fewer = []
+        for at in range(1, len(nodes), 2):
+            low, j = nodes[at - 1], nodes[at]
+            high = nodes[at + 1] if at + 1 < len(nodes) else None
+            m, a = masses[j], links[at - 1]
+            b = links[at] if high is not None else None
+            p = 1.0 / (m + a if high is None else m + (a + b))
+            g = a * p
+            h = None if high is None else b * p
+            steps.append((low, j, high, p, g, h))
+            masses[low] += g * m
+            if high is not None:
+                masses[high] += h * m
+                fewer.append(g * b)
+        nodes, links = nodes[::2], fewer
+    return steps, 1.0 / masses[0]
+
+
+def chain_solve(steps, last, right, count):
+    values = [right(j) for j in range(count)]
+    kept = []
+    for low, j, high, p, g, h in steps:
+        r = values[j]
+        kept.append(p * r)
+        values[low] += g * r
+        if high is not None:
+            values[high] += h * r
+    values[0] = last * values[0]
+    for (low, j, high, p, g, h), q in zip(reversed(steps), reversed(kept)):
+        q = q + g * values[low]
+        values[j] = q if high is None else q + h * values[high]
     return values
 
 
 def kernel(
-    fields_hbm, level_hbm, spread, out,
-    field, level, visc, xg, xh, xq, xa, xb, xp, half, yg, yh, yq, ya, yb, yp,
+    fields_hbm, level_hbm, spread_hbm, out,
+    spread, field, level, visc, xg, xh, xq, xa, xb, xp, half, yg, yh, yq, ya, yb, yp,
     *rest,
 ):
     gx, gy = lax.axis_index("gx"), lax.axis_index("gy")
     count = len(MESSAGES)
     sends = dict(zip(MESSAGES, rest[:count]))
     recvs = dict(zip(MESSAGES, rest[count : 2 * count]))
-    chain_p, chain_h, send_sem, recv_sem, in_sem = rest[2 * count :]
+    chain_p, chain_g, chain_h, send_sem, recv_sem, in_sem = rest[2 * count :]
     everyone = partners("gx", gx, gy) + partners("gy", gx, gy)
     hops = [ring(i, 4) + ring(j, 4) for i, j in X_STEPS] + [ring(i, 8) for i, j in Y_STEPS]
     greeted = [everyone[k] for k in sorted(range(len(everyone)), key=lambda k: -hops[k])]
@@ -124,7 +122,9 @@
         pl.semaphore_signal(barrier, inc=1, device_id=device, device_id_type=MESH)
     level_in = pltpu.make_async_copy(level_hbm, level, in_sem.at[0])
     fields_in = pltpu.make_async_copy(fields_hbm, field, in_sem.at[1])
+    spread_in = pltpu.make_async_copy(spread_hbm, spread, in_sem.at[2])
     level_in.start()
+    spread_in.start()
     fields_in.start()
 
     x_order = [(peer, gy) for peer in others(X_FIRST, gx)]
@@ -167,6 +167,7 @@
     def peer_rows(what, k, row, count=8):
         return rows(k * MESSAGES[what][2] + row, count)
 
+    spread_in.wait()
     rate = [2500.0 * spread[f] for f in range(FIELDS)]
     zero = jnp.zeros((16, LANES), jnp.float32)
     one = jnp.ones((16, LANES), jnp.float32)
@@ -325,14 +326,16 @@
             return rate_x * (end_visc(j // 2, 1) + end_visc(j // 2 + 1, 0))
 
         total(what).wait_recv()
-        parts = chain_matrix(
+        steps, last = chain_matrix(
             lambda j: recvs[what][peer_rows(what, j // 2, n * (j % 2))],
             link,
             2.0 * rate_x * end_visc(0, 0),
             2.0 * rate_x * end_visc(PEERS - 1, 1),
-            PEERS,
+            2 * PEERS,
         )
-        solved = chain_solve(parts, lambda j: recvs[what][peer_rows(what, j // 2, n * (3 + j % 2))], PEERS)
+        solved = chain_solve(
+            steps, last, lambda j: recvs[what][peer_rows(what, j // 2, n * (3 + j % 2))], 2 * PEERS
+        )
         back = ("xv", g)
         for k in range(PEERS):
             for v in range(2):
@@ -365,7 +368,7 @@
     lax.fori_loop(0, NY - 2, backward, ((zero, one),) * FIELDS)
 
     total("ym").wait_recv()
-    middles = []
+    y_steps, y_last = [], []
     for g, group in enumerate(GROUPS):
         n = len(group)
         rate_y = rates(group, 1)
@@ -378,19 +381,19 @@
                 return recvs["ym"][peer_rows("ym", j // 2, y_at[g] + 2 * n)]
             return rate_y * (end_visc(j // 2, 1) + end_visc(j // 2 + 1, 0))
 
-        low, high, middle = chain_matrix(
+        steps, last = chain_matrix(
             lambda j: recvs["ym"][peer_rows("ym", j // 2, y_at[g] + n * (j % 2))],
             link,
             2.0 * rate_y * end_visc(0, 0),
             2.0 * rate_y * end_visc(PEERS - 1, 1),
-            PEERS,
+            2 * PEERS,
         )
-        middles.append(middle)
-        for side, steps in enumerate((low, high)):
-            for j, (p, h) in enumerate(steps):
-                at = rows(((2 * g + side) * PEERS + j) * 8, 8)
-                chain_p[at] = p
-                chain_h[at] = h
+        y_last.append(last)
+        y_steps.append([(low, j, high) for low, j, high, *values in steps])
+        for low, j, high, *values in steps:
+            for kept, value in zip((chain_p, chain_g, chain_h), values):
+                if value is not None:
+                    kept[rows((2 * g * PEERS + j) * 8, 8)] = value
 
     for g, group in enumerate(GROUPS):
         what, back, n = ("yr", g), ("xv", g), len(group)
@@ -413,7 +416,7 @@
                 sends[what][peer_rows(what, i, n + place, 1)] = high
                 return carry
 
-            lax.fori_loop(0, NX, finish_x, 0, unroll=8)
+            lax.fori_loop(0, NX, finish_x, 0, unroll=16)
         send(what)
         keep(what)
 
@@ -441,13 +444,13 @@
 
     for g, group in enumerate(GROUPS):
         what, back, n = ("yr", g), ("yv", g), len(group)
-        parts = []
-        for side in range(2):
-            at = [rows(((2 * g + side) * PEERS + j) * 8, 8) for j in range(PEERS - 1)]
-            parts.append([(chain_p[place], chain_h[place]) for place in at])
         total(what).wait_recv()
+        steps = [
+            (low, j, high, *(kept[rows((2 * g * PEERS + j) * 8, 8)] for kept in (chain_p, chain_g, chain_h)))
+            for low, j, high in y_steps[g]
+        ]
         solved = chain_solve(
-            (*parts, middles[g]), lambda j: recvs[what][peer_rows(what, j // 2, n * (j % 2))], PEERS
+            steps, y_last[g], lambda j: recvs[what][peer_rows(what, j // 2, n * (j % 2))], 2 * PEERS
         )
         for k in range(PEERS):
             for v in range(2):
@@ -467,7 +470,7 @@
                 out[at] = yp[at] + ya[at] * low_end + yb[at] * high_end
             return carry
 
-        lax.fori_loop(0, NX, finish_y, 0, unroll=2)
+        lax.fori_loop(0, NX, finish_y, 0, unroll=4)
     for what in MESSAGES:
         total(what).wait_send()
 
@@ -485,19 +488,20 @@
         in_specs=[
             pl.BlockSpec(memory_space=pl.ANY),
             pl.BlockSpec(memory_space=pl.ANY),
-            pl.BlockSpec(memory_space=pltpu.SMEM),
+            pl.BlockSpec(memory_space=pl.ANY),
         ],
         out_specs=pl.BlockSpec(memory_space=pltpu.VMEM),
-        scratch_shapes=[whole, buffer(ROWS), buffer(ROWS)]
+        scratch_shapes=[pltpu.SMEM((FIELDS,), jnp.float32), whole, buffer(ROWS), buffer(ROWS)]
         + [whole] * 13
         + messages
         + arrivals
         + [
             buffer(2 * len(GROUPS) * PEERS * 8),
             buffer(2 * len(GROUPS) * PEERS * 8),
+            buffer(2 * len(GROUPS) * PEERS * 8),
             pltpu.SemaphoreType.DMA((len(MESSAGES),)),
             pltpu.SemaphoreType.DMA((len(MESSAGES),)),
-            pltpu.SemaphoreType.DMA((2,)),
+            pltpu.SemaphoreType.DMA((3,)),
         ],
         compiler_params=pltpu.CompilerParams(
             collective_id=0, has_side_effects=True, vmem_limit_bytes=60 * 1024 * 1024

time: 34.4 us -> 33.5 us (0.974)
  Pallas kernels: 33.2 us -> 32.4 us
    pallas_call x1, Pallas kernels: 33.2 us -> 32.4 us  [shards(): pl.pallas_call(kernel, out_shape=pltpu.VMEM((FIELDS * ROWS, LANES), jnp.f...]
where the time goes in v5:
time: 33.5 us; the launch traced here: 33.4 us
  Pallas kernels  32.4 us (97%)
  local copies, waits for them, and re-layouts  1.06 us (3%)
    pallas_call x1, Pallas kernels, shards(): pl.pallas_call(kernel, out_shape=pltpu.VMEM((FIELDS * ROWS, LANES), jnp.f...  32.4 us
    unnamed x1, local copies, waits for them, and re-layouts  1.06 us

profile of v5, /device:TPU:1, one launch (start us, length us, event | category | flops | bytes accessed | tf_op | source)
XLA Modules:
  0.0 33.4 jit_solution(10565086290762834183)
XLA Ops:
  0.0 32.4 %shard_map.37 = f32[2560,128]{1,0:T(8,128)S(1)} custom-call(f32[2560,128]{1,0:T(8,128)} %bitcast.4, f32[512,128]{1,0:T(8,128)} %bitcast.5, f32[5]{0:T(128)} %spread_hbm.1), custom_call_target="tpu_custom_call" | custom-call | tf_op jit(solution)/shard_map/pallas_call | solution.py:485
  32.4 1.1 %copy.5 = f32[5,16,32,128]{3,2,1,0:T(8,128)} copy(f32[5,16,32,128]{3,2,1,0:T(8,128)S(1)} %bitcast.3) | data formatting | bytes 2621440

commit v6 on v5

--- a/solution.py
+++ b/solution.py
@@ -112,14 +112,24 @@
     count = len(MESSAGES)
     sends = dict(zip(MESSAGES, rest[:count]))
     recvs = dict(zip(MESSAGES, rest[count : 2 * count]))
-    chain_p, chain_g, chain_h, send_sem, recv_sem, in_sem = rest[2 * count :]
+    chain_p, chain_g, chain_h, send_sem, recv_sem, in_sem, line_sem, all_sem = rest[2 * count :]
     everyone = partners("gx", gx, gy) + partners("gy", gx, gy)
-    hops = [ring(i, 4) + ring(j, 4) for i, j in X_STEPS] + [ring(i, 8) for i, j in Y_STEPS]
-    greeted = [everyone[k] for k in sorted(range(len(everyone)), key=lambda k: -hops[k])]
+
+    front = gx < 4
+    my_line = [(((gx + 4 * i) & 12) + (gx & 3), gy) for i in (2, 1, 3)]
+    x_partners, y_partners = partners("gx", gx, gy), partners("gy", gx, gy)
+
+    def tell(sem, devices):
+        for device in devices:
+            pl.semaphore_signal(sem, inc=1, device_id=device, device_id_type=MESH)
 
     barrier = pltpu.get_barrier_semaphore()
-    for device in greeted:
-        pl.semaphore_signal(barrier, inc=1, device_id=device, device_id_type=MESH)
+    tell(barrier, x_partners)
+
+    @pl.when(front)
+    def _():
+        tell(barrier, y_partners)
+
     level_in = pltpu.make_async_copy(level_hbm, level, in_sem.at[0])
     fields_in = pltpu.make_async_copy(fields_hbm, field, in_sem.at[1])
     spread_in = pltpu.make_async_copy(spread_hbm, spread, in_sem.at[2])
@@ -236,9 +246,14 @@
         sends[what][share(what, n + s)] = nu0
         sends[what][share(what, n + 2 + s)] = nu
 
-    pl.semaphore_wait(barrier, len(everyone))
+    pl.semaphore_wait(barrier, jnp.where(front, len(everyone), len(x_partners)))
     for g in range(len(GROUPS)):
         send(("xo", g))
+
+    @pl.when(front)
+    def _():
+        tell(line_sem, y_partners)
+
     for g in range(len(GROUPS)):
         keep(("xo", g))
 
@@ -280,7 +295,6 @@
                 at += 1
     sends["ym"][share("ym", at)] = nu0
     sends["ym"][share("ym", at + 1)] = nu
-    send("ym")
     keep("ym")
 
     for s in range(2):
@@ -302,6 +316,11 @@
             return tuple(new)
 
         lax.fori_loop(0, NX - 2, backward, ((zero, one, zero),) * FIELDS)
+
+    @pl.when(front)
+    def _():
+        pl.semaphore_wait(line_sem, len(y_partners))
+        tell(all_sem, my_line)
 
     line = lax.broadcasted_iota(jnp.int32, (8, LANES), 0)
 
@@ -345,6 +364,12 @@
     for g in range(len(GROUPS)):
         send(("xv", g), x_order[7:])
 
+    @pl.when(jnp.logical_not(front))
+    def _():
+        pl.semaphore_wait(all_sem, 1)
+
+    send("ym")
+
     def natural(f, j):
         return pl.ds(f * ROWS + j, 16, stride=NY)
 
@@ -366,6 +391,53 @@
         return tuple(new)
 
     lax.fori_loop(0, NY - 2, backward, ((zero, one),) * FIELDS)
+
+    for g, group in enumerate(GROUPS):
+        what, back, n = ("yr", g), ("xv", g), len(group)
+        total(back).wait_recv()
+        for place, f in enumerate(group):
+            low_end, high_end = (
+                jnp.concatenate(
+                    [recvs[back][share(back, 2 * n * v + 2 * place + s)] for s in range(2)], axis=0
+                )
+                for v in range(2)
+            )
+
+            def finish_x(i, carry, f=f, place=place, low_end=low_end, high_end=high_end):
+                at = rows(pl.multiple_of(f * ROWS + i * NY, NY), NY)
+                value = xp[at] + xa[at] * low_end + xb[at] * high_end
+                half[at] = value
+                low = jnp.sum(ya[at] * value, axis=0, keepdims=True)
+                high = jnp.sum(yb[at] * value, axis=0, keepdims=True)
+                sends[what][peer_rows(what, i, place, 1)] = low
+                sends[what][peer_rows(what, i, n + place, 1)] = high
+                return carry
+
+            lax.fori_loop(0, NX, finish_x, 0, unroll=16)
+        send(what)
+        keep(what)
+
+    def forward(j, right):
+        new = []
+        for f in range(FIELDS):
+            at = y_row(f, j)
+            yg[at] = yq[at] * right[f]
+            new.append(half[natural(f, j + 1)] + yh[at] * right[f])
+        return tuple(new)
+
+    lax.fori_loop(1, NY - 1, forward, tuple(half[natural(f, 1)] for f in range(FIELDS)))
+
+    def backward(k, state):
+        j = NY - 2 - k
+        new = []
+        for f in range(FIELDS):
+            at = y_row(f, j)
+            p = yg[at] + yh[at] * state[f]
+            yp[natural(f, j)] = p
+            new.append(p)
+        return tuple(new)
+
+    lax.fori_loop(0, NY - 2, backward, (zero,) * FIELDS)
 
     total("ym").wait_recv()
     y_steps, y_last = [], []
@@ -394,53 +466,6 @@
             for kept, value in zip((chain_p, chain_g, chain_h), values):
                 if value is not None:
                     kept[rows((2 * g * PEERS + j) * 8, 8)] = value
-
-    for g, group in enumerate(GROUPS):
-        what, back, n = ("yr", g), ("xv", g), len(group)
-        total(back).wait_recv()
-        for place, f in enumerate(group):
-            low_end, high_end = (
-                jnp.concatenate(
-                    [recvs[back][share(back, 2 * n * v + 2 * place + s)] for s in range(2)], axis=0
-                )
-                for v in range(2)
-            )
-
-            def finish_x(i, carry, f=f, place=place, low_end=low_end, high_end=high_end):
-                at = rows(pl.multiple_of(f * ROWS + i * NY, NY), NY)
-                value = xp[at] + xa[at] * low_end + xb[at] * high_end
-                half[at] = value
-                low = jnp.sum(ya[at] * value, axis=0, keepdims=True)
-                high = jnp.sum(yb[at] * value, axis=0, keepdims=True)
-                sends[what][peer_rows(what, i, place, 1)] = low
-                sends[what][peer_rows(what, i, n + place, 1)] = high
-                return carry
-
-            lax.fori_loop(0, NX, finish_x, 0, unroll=16)
-        send(what)
-        keep(what)
-
-    def forward(j, right):
-        new = []
-        for f in range(FIELDS):
-            at = y_row(f, j)
-            yg[at] = yq[at] * right[f]
-            new.append(half[natural(f, j + 1)] + yh[at] * right[f])
-        return tuple(new)
-
-    lax.fori_loop(1, NY - 1, forward, tuple(half[natural(f, 1)] for f in range(FIELDS)))
-
-    def backward(k, state):
-        j = NY - 2 - k
-        new = []
-        for f in range(FIELDS):
-            at = y_row(f, j)
-            p = yg[at] + yh[at] * state[f]
-            yp[natural(f, j)] = p
-            new.append(p)
-        return tuple(new)
-
-    lax.fori_loop(0, NY - 2, backward, (zero,) * FIELDS)
 
     for g, group in enumerate(GROUPS):
         what, back, n = ("yr", g), ("yv", g), len(group)
@@ -502,7 +527,8 @@
             pltpu.SemaphoreType.DMA((len(MESSAGES),)),
             pltpu.SemaphoreType.DMA((len(MESSAGES),)),
             pltpu.SemaphoreType.DMA((3,)),
-        ],
+        ]
+        + [pltpu.SemaphoreType.REGULAR] * 2,
         compiler_params=pltpu.CompilerParams(
             collective_id=0, has_side_effects=True, vmem_limit_bytes=60 * 1024 * 1024
         ),

time: 33.5 us -> 32.9 us (0.982)
  Pallas kernels: 32.4 us -> 31.7 us
    pallas_call x1, Pallas kernels: 32.4 us -> 31.7 us  [shards(): pl.pallas_call(kernel, out_shape=pltpu.VMEM((FIELDS * ROWS, LANES), jnp.f...]
where the time goes in v6:
time: 32.9 us; the launch traced here: 32.8 us
  Pallas kernels  31.7 us (96%)
  local copies, waits for them, and re-layouts  1.06 us (3%)
    pallas_call x1, Pallas kernels, shards(): pl.pallas_call(kernel, out_shape=pltpu.VMEM((FIELDS * ROWS, LANES), jnp.f...  31.7 us
    unnamed x1, local copies, waits for them, and re-layouts  1.06 us

profile of v6, /device:TPU:1, one launch (start us, length us, event | category | flops | bytes accessed | tf_op | source)
XLA Modules:
  0.0 32.8 jit_solution(3614934348561030148)
XLA Ops:
  0.0 31.7 %shard_map.37 = f32[2560,128]{1,0:T(8,128)S(1)} custom-call(f32[2560,128]{1,0:T(8,128)} %bitcast.4, f32[512,128]{1,0:T(8,128)} %bitcast.5, f32[5]{0:T(128)} %spread_hbm.1), custom_call_target="tpu_custom_call" | custom-call | tf_op jit(solution)/shard_map/pallas_call | solution.py:510
  31.7 1.1 %copy.5 = f32[5,16,32,128]{3,2,1,0:T(8,128)} copy(f32[5,16,32,128]{3,2,1,0:T(8,128)S(1)} %bitcast.3) | data formatting | bytes 2621440

commit v7 on v6

--- a/solution.py
+++ b/solution.py
@@ -504,9 +504,9 @@
     def buffer(count):
         return pltpu.VMEM((count, LANES), jnp.float32)
 
-    whole = buffer(FIELDS * ROWS)
-    messages = [buffer(PEERS * size) for axis, count, size in MESSAGES.values()]
-    arrivals = [buffer(PEERS * size + 8) for axis, count, size in MESSAGES.values()]
+    whole = buffer(FIELDS * ROWS + NY)
+    messages = [buffer((PEERS + 1) * size) for axis, count, size in MESSAGES.values()]
+    arrivals = [buffer((PEERS + 1) * size) for axis, count, size in MESSAGES.values()]
     solved = pl.pallas_call(
         kernel,
         out_shape=pltpu.VMEM((FIELDS * ROWS, LANES), jnp.float32),
@@ -516,7 +516,7 @@
             pl.BlockSpec(memory_space=pl.ANY),
         ],
         out_specs=pl.BlockSpec(memory_space=pltpu.VMEM),
-        scratch_shapes=[pltpu.SMEM((FIELDS,), jnp.float32), whole, buffer(ROWS), buffer(ROWS)]
+        scratch_shapes=[pltpu.SMEM((FIELDS,), jnp.float32), buffer(FIELDS * ROWS), buffer(ROWS), buffer(ROWS + NY)]
         + [whole] * 13
         + messages
         + arrivals

time: 32.9 us -> 32.9 us (level)
  no operation moved by 1% of the time
where the time goes in v7:
time: 32.9 us; the launch traced here: 32.8 us
  Pallas kernels  31.7 us (96%)
  local copies, waits for them, and re-layouts  1.06 us (3%)
    pallas_call x1, Pallas kernels, shards(): pl.pallas_call(kernel, out_shape=pltpu.VMEM((FIELDS * ROWS, LANES), jnp.f...  31.7 us
    unnamed x1, local copies, waits for them, and re-layouts  1.06 us

profile of v7, /device:TPU:1, one launch (start us, length us, event | category | flops | bytes accessed | tf_op | source)
XLA Modules:
  0.0 32.8 jit_solution(6967256442626925344)
XLA Ops:
  0.0 31.7 %shard_map.37 = f32[2560,128]{1,0:T(8,128)S(1)} custom-call(f32[2560,128]{1,0:T(8,128)} %bitcast.4, f32[512,128]{1,0:T(8,128)} %bitcast.5, f32[5]{0:T(128)} %spread_hbm.1), custom_call_target="tpu_custom_call" | custom-call | tf_op jit(solution)/shard_map/pallas_call | solution.py:510
  31.7 1.1 %copy.5 = f32[5,16,32,128]{3,2,1,0:T(8,128)} copy(f32[5,16,32,128]{3,2,1,0:T(8,128)S(1)} %bitcast.3) | data formatting | bytes 2621440

commit v8 on v7

--- a/solution.py
+++ b/solution.py
@@ -480,8 +480,10 @@
         for k in range(PEERS):
             for v in range(2):
                 sends[back][peer_rows(back, k, n * v, n)] = solved[2 * k + v][:n]
-        send(back, y_order)
+        send(back, y_order[:1])
         keep(back)
+    for g in range(len(GROUPS)):
+        send(("yv", g), y_order[1:])
 
     for g, group in enumerate(GROUPS):
         back, n = ("yv", g), len(group)

time: 32.9 us -> 32.9 us (level)
  no operation moved by 1% of the time
where the time goes in v8:
time: 32.9 us; the launch traced here: 32.8 us
  Pallas kernels  31.7 us (96%)
  local copies, waits for them, and re-layouts  1.06 us (3%)
    pallas_call x1, Pallas kernels, shards(): pl.pallas_call(kernel, out_shape=pltpu.VMEM((FIELDS * ROWS, LANES), jnp.f...  31.7 us
    unnamed x1, local copies, waits for them, and re-layouts  1.06 us

profile of v8, /device:TPU:1, one launch (start us, length us, event | category | flops | bytes accessed | tf_op | source)
XLA Modules:
  0.0 32.8 jit_solution(5622103947133478969)
XLA Ops:
  0.0 31.7 %shard_map.37 = f32[2560,128]{1,0:T(8,128)S(1)} custom-call(f32[2560,128]{1,0:T(8,128)} %bitcast.4, f32[512,128]{1,0:T(8,128)} %bitcast.5, f32[5]{0:T(128)} %spread_hbm.1), custom_call_target="tpu_custom_call" | custom-call | tf_op jit(solution)/shard_map/pallas_call | solution.py:512
  31.7 1.1 %copy.5 = f32[5,16,32,128]{3,2,1,0:T(8,128)} copy(f32[5,16,32,128]{3,2,1,0:T(8,128)S(1)} %bitcast.3) | data formatting | bytes 2621440
